TPU v7x, 32 devices: a whole 2x2x4 slice. The times are simulated.
32 devices in a mesh: seq: 8 (over z, core), fsdp: 4 (over y, x).
Axes of the slice: x: 2, y: 2, z: 4, core: 2. Of those that a mesh axis runs over, the one named last changes fastest.
Arguments:
- tokens: bfloat16 [4, 2048, 1536], P('fsdp', 'seq'), may hold values from -6 to 6
- positions: int32 [4, 2048], P('fsdp', 'seq'), may hold values from 0 to 3839, as said below
- first_gain: bfloat16 [1536], P('fsdp'), may hold values from 0.5 to 1.5
- query_weight: bfloat16 [1536, 1536], P('fsdp'), may hold values from -0.15625 to 0.15625
- key_weight: bfloat16 [1536, 768], P('fsdp'), may hold values from -0.15625 to 0.15625
- value_weight: bfloat16 [1536, 768], P('fsdp'), may hold values from -0.15625 to 0.15625
- output_weight: bfloat16 [1536, 1536], P('fsdp'), may hold values from -6 to 6
- second_gain: bfloat16 [1536], P('fsdp'), may hold values from 0.5 to 1.5
- gate_weight: bfloat16 [1536, 4096], P('fsdp'), may hold values from -0.15625 to 0.15625
- up_weight: bfloat16 [1536, 4096], P('fsdp'), may hold values from -0.15625 to 0.15625
- down_weight: bfloat16 [4096, 1536], P('fsdp'), may hold values from -0.09375 to 0.09375
- cotangent: bfloat16 [4, 2048, 1536], P('fsdp', 'seq'), may hold values from -6 to 6
Outputs:
- block_output: bfloat16 [4, 2048, 1536], P('fsdp', 'seq')
- input_grad: bfloat16 [4, 2048, 1536], P('fsdp', 'seq')
- first_gain_grad: float32 [1536], P('fsdp')
- query_grad: float32 [1536, 1536], P('fsdp')
- key_grad: float32 [1536, 768], P('fsdp')
- value_grad: float32 [1536, 768], P('fsdp')
- output_grad: float32 [1536, 1536], P('fsdp')
- second_gain_grad: float32 [1536], P('fsdp')
- gate_grad: float32 [1536, 4096], P('fsdp')
- up_grad: float32 [1536, 4096], P('fsdp')
- down_grad: float32 [4096, 1536], P('fsdp')
Inputs may be any that keep to these rules, and one draw needn't show every extreme that they name: Each sequence is a pack of three documents; positions count from 0 at each document's first token; the middle document begins within the sequence's first 256 tokens, after its first token, and holds exactly 3840 tokens.
All inputs are finite; a program needn't handle non-finite values.
Results may differ from a plain program's by a relative error of at most 0.02.
Values may be sent and summed in bfloat16 or wider, within the bound.
No kernel may reach another device: no remote copies, remote signals or barrier semaphores. Data moves between devices by JAX's collectives and lax.ppermute only.
A program may use at most 320 MiB of HBM per device.

v0:
```python
import functools
import math

import jax
import jax.numpy as jnp
from jax import lax
from jax.experimental import pallas as pl
from jax.experimental.pallas import tpu as pltpu
from jax.sharding import Mesh
from jax.sharding import PartitionSpec as P

QH = 16
KVH = 8
HD = 96


THETA = 100000.0
EPS = 1e-05
LOW = jnp.bfloat16
F32 = jnp.float32
NEG = -1e30
LN2 = math.log(2.0)


def contract(left, right, left_axis, right_axis):
    return lax.dot_general(
        left, right, (((left_axis,), (right_axis,)), ((), ())), preferred_element_type=F32
    )


def visible(first, second, query_block, key_block, size):
    key = key_block * size + lax.broadcasted_iota(jnp.int32, (size, size), 0)
    query = query_block * size + lax.broadcasted_iota(jnp.int32, (1, size), 1)
    start = jnp.where(query >= second, second, jnp.where(query >= first, first, 0))
    return (key >= start) & (key <= query)


def slot_of(block, count):
    return (block % (count // 2)) * 2 + block // (count // 2)


def forward_kernel(
    scalars,
    own_ref,
    other_ref,
    low_ref,
    full_ref,
    log_ref,
    query_s,
    key_s,
    value_s,
    top_s,
    total_s,
    mixed_s,
    *,
    size,
    count,
):
    half = scalars[0]
    first = scalars[1]
    second = scalars[2]
    here = pl.program_id(0)
    per_half = count // 2

    @pl.when(here == 0)
    def _():
        for ref, side in ((own_ref, half), (other_ref, 1 - half)):
            for step in range(per_half):
                block = side * per_half + step
                columns = slice(step * size, (step + 1) * size)
                query_s[block] = ref[0:HD, columns]
                key_s[block] = ref[HD : 2 * HD, columns].T
                value_s[block] = ref[2 * HD : 3 * HD, columns]

    query = query_s[here]
    top_s[...] = jnp.full_like(top_s, NEG)
    total_s[...] = jnp.zeros_like(total_s)
    mixed_s[...] = jnp.zeros_like(mixed_s)

    def add_block(block, masked):
        scores = contract(key_s[block], query, 1, 0)
        if masked:
            scores = jnp.where(visible(first, second, here, block, size), scores, NEG)
        old_top = top_s[...]
        top = jnp.maximum(old_top, jnp.max(scores, 0, keepdims=True))
        expo = jnp.exp2(scores - top)
        scale = jnp.exp2(old_top - top)
        top_s[...] = top
        total_s[...] = total_s[...] * scale + jnp.sum(expo, 0, keepdims=True)
        mixed_s[...] = mixed_s[...] * scale + contract(value_s[block], expo.astype(LOW), 1, 0)

    last = count - 1

    @pl.loop(1, jnp.where(here == last, 1, here))
    def _(block):
        add_block(block, False)

    @pl.loop(0, jnp.where(here == last, count, jnp.minimum(here + 1, 2)))
    def _(step):
        add_block(jnp.where(here == last, step, step * here), True)

    total = total_s[...]
    result = mixed_s[...] / total
    full_ref[0] = result
    low_ref[0] = result.astype(LOW)
    log_ref[0] = top_s[...] + jnp.log2(total)


def backward_kernel(
    scalars,
    own_ref,
    other_ref,
    grad_ref,
    full_ref,
    log_ref,
    kept_ref,
    leaving_ref,
    query_s,
    key_s,
    value_s,
    delta_s,
    query_grad_s,
    key_grad_s,
    value_grad_s,
    *,
    size,
    count,
):
    half = scalars[0]
    first = scalars[1]
    second = scalars[2]
    here = pl.program_id(0)
    per_half = count // 2

    @pl.when(here == 0)
    def _():
        for ref, side in ((own_ref, half), (other_ref, 1 - half)):
            for step in range(per_half):
                block = side * per_half + step
                columns = slice(step * size, (step + 1) * size)
                query_s[block] = ref[0:HD, columns]
                key_s[block] = ref[HD : 2 * HD, columns]
                value_s[block] = ref[2 * HD : 3 * HD, columns].T
        for block in range(count):
            delta_s[block] = jnp.sum(
                grad_ref[slot_of(block, count)].astype(F32) * full_ref[block], 0, keepdims=True
            )
        query_grad_s[...] = jnp.zeros_like(query_grad_s)

    key_grad_s[...] = jnp.zeros_like(key_grad_s)
    value_grad_s[...] = jnp.zeros_like(value_grad_s)
    key = key_s[here]
    key_rows = key.T
    value_rows = value_s[here]

    def add_block(block, masked):
        query = query_s[block]
        grad = grad_ref[slot_of(block, count)]
        scores = contract(key_rows, query, 1, 0)
        if masked:
            scores = jnp.where(visible(first, second, block, here, size), scores, NEG)
        probs = jnp.exp2(scores - log_ref[block])
        grad_probs = contract(value_rows, grad, 1, 0)
        grad_scores = (probs * (grad_probs - delta_s[block])).astype(LOW)
        value_grad_s[...] += contract(grad, probs.astype(LOW), 1, 1)
        key_grad_s[...] += contract(query, grad_scores, 1, 1)
        query_grad_s[block] += contract(key, grad_scores, 1, 0)

    last = count - 1

    @pl.loop(here + 1, jnp.where(here == 0, 1, last))
    def _(block):
        add_block(block, False)

    @pl.loop(0, jnp.where(here == 0, count, jnp.where(here == last, 1, 2)))
    def _(step):
        add_block(jnp.where(here == 0, step, jnp.where(step == 0, here, last)), True)

    side = here // per_half
    columns = pl.ds(pl.multiple_of((here % per_half) * size, size), size)

    def write(out_ref):
        out_ref[0:HD, columns] = (query_grad_s[here] * HD**-0.5).astype(LOW)
        out_ref[HD : 2 * HD, columns] = (key_grad_s[...] * LN2).astype(LOW)
        out_ref[2 * HD : 3 * HD, columns] = value_grad_s[...].astype(LOW)

    @pl.when(side == half)
    def _():
        write(kept_ref)

    @pl.when(side != half)
    def _():
        write(leaving_ref)


def attend_forward(scalars, own, other, size):
    count = 2 * own.shape[1] // size
    whole = lambda shape: pl.BlockSpec(shape, lambda i, s: (0,) * len(shape))
    pairs = count * (count + 1) // 2
    return pl.pallas_call(
        functools.partial(forward_kernel, size=size, count=count),
        grid_spec=pltpu.PrefetchScalarGridSpec(
            num_scalar_prefetch=1,
            grid=(count,),
            in_specs=[whole(own.shape), whole(other.shape)],
            out_specs=[
                pl.BlockSpec(
                    (1, HD, size), lambda i, s: (slot_of(i, count), 0, 0)
                ),
                pl.BlockSpec((1, HD, size), lambda i, s: (i, 0, 0)),
                pl.BlockSpec((1, 1, size), lambda i, s: (i, 0, 0)),
            ],
            scratch_shapes=[
                pltpu.VMEM((count, HD, size), LOW),
                pltpu.VMEM((count, size, HD), LOW),
                pltpu.VMEM((count, HD, size), LOW),
                pltpu.VMEM((1, size), F32),
                pltpu.VMEM((1, size), F32),
                pltpu.VMEM((HD, size), F32),
            ],
        ),
        out_shape=[
            jax.ShapeDtypeStruct((count, HD, size), LOW),
            jax.ShapeDtypeStruct((count, HD, size), F32),
            jax.ShapeDtypeStruct((count, 1, size), F32),
        ],
        compiler_params=pltpu.CompilerParams(
            dimension_semantics=("arbitrary",), vmem_limit_bytes=32 * 2**20
        ),
        cost_estimate=pl.CostEstimate(
            flops=pairs * size * size * HD * 32,
            bytes_accessed=10 * 2**20,
            transcendentals=pairs * size * size,
        ),
        name="attend_forward",
    )(scalars, own, other)


def attend_backward(scalars, own, other, grad, full, log_total):
    count, _, size = grad.shape
    whole = lambda shape: pl.BlockSpec(shape, lambda i, s: (0,) * len(shape))
    pairs = count * (count + 1) // 2
    out_shape = own.shape
    return pl.pallas_call(
        functools.partial(backward_kernel, size=size, count=count),
        grid_spec=pltpu.PrefetchScalarGridSpec(
            num_scalar_prefetch=1,
            grid=(count,),
            in_specs=[
                whole(own.shape),
                whole(other.shape),
                whole(grad.shape),
                whole(full.shape),
                whole(log_total.shape),
            ],
            out_specs=[whole(out_shape)] * 2,
            scratch_shapes=[
                pltpu.VMEM((count, HD, size), LOW),
                pltpu.VMEM((count, HD, size), LOW),
                pltpu.VMEM((count, size, HD), LOW),
                pltpu.VMEM((count, 1, size), F32),
                pltpu.VMEM((count, HD, size), F32),
                pltpu.VMEM((HD, size), F32),
                pltpu.VMEM((HD, size), F32),
            ],
        ),
        out_shape=[jax.ShapeDtypeStruct(out_shape, LOW)] * 2,
        compiler_params=pltpu.CompilerParams(
            dimension_semantics=("arbitrary",), vmem_limit_bytes=32 * 2**20
        ),
        cost_estimate=pl.CostEstimate(
            flops=pairs * size * size * HD * 42,
            bytes_accessed=16 * 2**20,
            transcendentals=pairs * size * size,
        ),
        name="attend_backward",
    )(scalars, own, other, grad, full, log_total)


def place_rows_kernel(order, *refs):
    pieces, out_ref = refs[:-1], refs[-1]
    size = pieces[0].shape[0]
    for index, piece in enumerate(pieces):
        start = pl.multiple_of(order[index] * size, size)
        out_ref[pl.ds(start, size), :] = piece[...].astype(F32)


def place_rows(order, pieces):
    size, width = pieces[0].shape
    total = size * len(pieces)
    step = 512
    return pl.pallas_call(
        place_rows_kernel,
        grid_spec=pltpu.PrefetchScalarGridSpec(
            num_scalar_prefetch=1,
            grid=(width // step,),
            in_specs=[pl.BlockSpec((size, step), lambda i, s: (0, i)) for _ in pieces],
            out_specs=pl.BlockSpec((total, step), lambda i, s: (0, i)),
        ),
        out_shape=jax.ShapeDtypeStruct((total, width), F32),
        compiler_params=pltpu.CompilerParams(vmem_limit_bytes=24 * 2**20),
        cost_estimate=pl.CostEstimate(
            flops=0, bytes_accessed=total * width * 6, transcendentals=0
        ),
        name="place_rows",
    )(order, *pieces)


def place_columns_kernel(order, gain_ref, gate_w_ref, up_w_ref, *refs):
    count = (len(refs) - 3) // 2
    gates, ups = refs[:count], refs[count : 2 * count]
    gate_ref, up_ref, sum_ref = refs[2 * count :]
    size = gates[0].shape[1]
    gain = gain_ref[...]
    total = jnp.zeros((gate_ref.shape[0], size), F32)
    for index in range(count):
        columns = pl.ds(pl.multiple_of(order[index] * size, size), size)
        gate, up = gates[index][...].astype(F32), ups[index][...].astype(F32)
        total += gate * gate_w_ref[:, columns].astype(F32)
        total += up * up_w_ref[:, columns].astype(F32)
        gate_ref[:, columns] = gate * gain
        up_ref[:, columns] = up * gain

    @pl.when(pl.program_id(0) == 0)
    def _():
        sum_ref[...] = jnp.zeros_like(sum_ref)

    sum_ref[...] += jnp.sum(total, 1, keepdims=True)


def place_columns(order, gain, gate_weight, up_weight, gates, ups, shards):
    rows, width = gate_weight.shape
    span = width // shards
    size = span // len(gates)
    wide = pl.BlockSpec((rows, span), lambda i, s: (0, i))
    thin = pl.BlockSpec((rows, 1), lambda i, s: (0, 0))
    pieces = [pl.BlockSpec((rows, size), lambda i, s: (0, i)) for _ in (*gates, *ups)]
    return pl.pallas_call(
        place_columns_kernel,
        grid_spec=pltpu.PrefetchScalarGridSpec(
            num_scalar_prefetch=1,
            grid=(shards,),
            in_specs=[thin, wide, wide, *pieces],
            out_specs=[wide, wide, thin],
        ),
        out_shape=[
            jax.ShapeDtypeStruct((rows, width), F32),
            jax.ShapeDtypeStruct((rows, width), F32),
            jax.ShapeDtypeStruct((rows, 1), F32),
        ],
        compiler_params=pltpu.CompilerParams(
            dimension_semantics=("arbitrary",), vmem_limit_bytes=24 * 2**20
        ),
        cost_estimate=pl.CostEstimate(
            flops=rows * width * 6, bytes_accessed=rows * width * 16, transcendentals=0
        ),
        name="place_columns",
    )(order, gain, gate_weight, up_weight, *gates, *ups)


def place_heads_kernel(gain_ref, query_w, key_w, value_w, all_ref, query_ref, key_ref, value_ref, sum_ref):
    rows = gain_ref.shape[0]
    wide = query_ref.shape[1] // KVH
    gain = gain_ref[...]
    total = jnp.zeros((rows, 4 * HD), F32)
    pieces = [all_ref[i * rows : (i + 1) * rows, :].astype(F32) for i in range(KVH)]
    for start in range(0, KVH, 2):
        value = jnp.concatenate([piece[:, :wide] for piece in pieces[start : start + 2]], 1)
        columns = slice(start * wide, (start + 2) * wide)
        total += value * query_w[:, columns].astype(F32)
        query_ref[:, columns] = value * gain
    for first, weight, out_ref in ((wide, key_w, key_ref), (wide + HD, value_w, value_ref)):
        for start in range(0, KVH, 4):
            value = jnp.concatenate(
                [piece[:, first : first + HD] for piece in pieces[start : start + 4]], 1
            )
            columns = slice(start * HD, (start + 4) * HD)
            total += value * weight[:, columns].astype(F32)
            out_ref[:, columns] = value * gain
    sum_ref[...] = jnp.sum(total, 1, keepdims=True)


def place_heads(gain, query_weight, key_weight, value_weight, pieces):
    weights = (query_weight, key_weight, value_weight)
    rows = gain.shape[0]
    return pl.pallas_call(
        place_heads_kernel,
        out_shape=[jax.ShapeDtypeStruct(weight.shape, F32) for weight in weights]
        + [jax.ShapeDtypeStruct((rows, 1), F32)],
        compiler_params=pltpu.CompilerParams(vmem_limit_bytes=32 * 2**20),
        cost_estimate=pl.CostEstimate(
            flops=rows * 3072 * 4, bytes_accessed=rows * 3072 * 8, transcendentals=0
        ),
        name="place_heads",
    )(gain, *weights, pieces)


def merge_kernel(scalars, kept_ref, came_ref, cosine_ref, sine_ref, out_ref, split_ref):
    lead = scalars[0] == 0
    lines, _, size = split_ref.shape
    for line in range(lines):
        columns = slice(line * size, (line + 1) * size)
        kept = kept_ref[:, columns].astype(F32)
        came = came_ref[:, columns].astype(F32)
        cosine, sine = cosine_ref[:, columns], sine_ref[:, columns]
        joint = kept[HD:] + came[HD:]
        first = jnp.where(lead, kept[:HD], came[:HD])
        second = jnp.where(lead, came[:HD], kept[:HD])
        turned = []
        for value in (first, second, joint[:HD]):
            low, high = value[: HD // 2], value[HD // 2 :]
            turned.append(low * cosine + high * sine)
            turned.append(high * cosine - low * sine)
        turned.append(joint[HD:])
        result = jnp.concatenate([part.astype(LOW) for part in turned], 0)
        out_ref[:, columns] = result
        split_ref[line] = result


def merge(scalars, kept, came, cosine, sine, lines):
    tokens = kept.shape[1]
    whole = lambda value: pl.BlockSpec(value.shape, lambda i, s: (0,) * len(value.shape))
    outs = [
        jax.ShapeDtypeStruct((4 * HD, tokens), LOW),
        jax.ShapeDtypeStruct((lines, 4 * HD, tokens // lines), LOW),
    ]
    return pl.pallas_call(
        merge_kernel,
        grid_spec=pltpu.PrefetchScalarGridSpec(
            num_scalar_prefetch=1,
            grid=(1,),
            in_specs=[whole(value) for value in (kept, came, cosine, sine)],
            out_specs=[whole(value) for value in outs],
        ),
        out_shape=outs,
        compiler_params=pltpu.CompilerParams(vmem_limit_bytes=24 * 2**20),
        cost_estimate=pl.CostEstimate(
            flops=tokens * HD * 24, bytes_accessed=tokens * HD * 30, transcendentals=0
        ),
        name="merge",
    )(scalars, kept, came, cosine, sine)


def pack_kernel(scalars, gain_ref, query_ref, key_ref, value_ref, *outs):
    core = scalars[3]
    gain = gain_ref[...]
    wide = query_ref.shape[1] // KVH
    span = wide + 2 * HD
    for which in range(2):

        @pl.when(core == which)
        def _():
            for line in range(KVH // 2):
                head = 2 * line + which
                value = jnp.concatenate(
                    [
                        query_ref[:, head * wide : (head + 1) * wide].astype(F32),
                        key_ref[:, head * HD : (head + 1) * HD].astype(F32),
                        value_ref[:, head * HD : (head + 1) * HD].astype(F32),
                    ],
                    1,
                )
                place = (line % 2) * span
                outs[line // 2][:, place : place + span] = (value * gain).astype(LOW)


def pack(scalars, gain, query_weight, key_weight, value_weight):
    rows, width = query_weight.shape
    whole = lambda value: pl.BlockSpec(value.shape, lambda i, s: (0, 0))
    weights = (gain, query_weight, key_weight, value_weight)
    outs = [jax.ShapeDtypeStruct((rows, width // 2), LOW)] * 2
    return pl.pallas_call(
        pack_kernel,
        grid_spec=pltpu.PrefetchScalarGridSpec(
            num_scalar_prefetch=1,
            grid=(1,),
            in_specs=[whole(value) for value in weights],
            out_specs=[whole(value) for value in outs],
        ),
        out_shape=outs,
        compiler_params=pltpu.CompilerParams(vmem_limit_bytes=24 * 2**20),
        cost_estimate=pl.CostEstimate(
            flops=rows * width, bytes_accessed=rows * width * 6, transcendentals=0
        ),
        name="pack",
    )(scalars, *weights)


def spread_kernel(scalars, lin_ref, cosine_ref, sine_ref, own_ref, leaving_ref):
    cosine, sine = cosine_ref[...], sine_ref[...]

    def turn(start, factor):
        low = lin_ref[start : start + HD // 2, :]
        high = lin_ref[start + HD // 2 : start + HD, :]
        turned = ((low * cosine - high * sine) * factor, (high * cosine + low * sine) * factor)
        return jnp.concatenate([part.astype(LOW) for part in turned], 0)

    lead = scalars[0] == 0
    first, second = turn(0, HD**-0.5 / LN2), turn(HD, HD**-0.5 / LN2)

    @pl.when(lead)
    def _():
        own_ref[0:HD] = first
        leaving_ref[0:HD] = second

    @pl.when(jnp.logical_not(lead))
    def _():
        own_ref[0:HD] = second
        leaving_ref[0:HD] = first

    key = turn(2 * HD, 1.0)
    value = lin_ref[3 * HD : 4 * HD].astype(LOW)
    for ref in (own_ref, leaving_ref):
        ref[HD : 2 * HD] = key
        ref[2 * HD : 3 * HD] = value


def spread(scalars, lin, cosine, sine):
    tokens = lin.shape[1]
    step = 512
    column = lambda rows: pl.BlockSpec((rows, step), lambda i, s: (0, i))
    return pl.pallas_call(
        spread_kernel,
        grid_spec=pltpu.PrefetchScalarGridSpec(
            num_scalar_prefetch=1,
            grid=(tokens // step,),
            in_specs=[column(4 * HD), column(HD // 2), column(HD // 2)],
            out_specs=[column(3 * HD)] * 2,
        ),
        out_shape=[jax.ShapeDtypeStruct((3 * HD, tokens), LOW)] * 2,
        compiler_params=pltpu.CompilerParams(vmem_limit_bytes=24 * 2**20),
        cost_estimate=pl.CostEstimate(
            flops=tokens * HD * 24, bytes_accessed=tokens * HD * 36, transcendentals=0
        ),
        name="spread",
    )(scalars, lin, cosine, sine)


def swap(value, axis):
    return lax.ppermute(value, axis, [(0, 1), (1, 0)])


def swap_near(value):
    return lax.ppermute(value, "z", [(0, 1), (1, 0), (2, 3), (3, 2)])


def swap_far(value):
    return lax.ppermute(value, "z", [(0, 2), (2, 0), (1, 3), (3, 1)])


def tie(*values):
    return lax.optimization_barrier(values)


def in_order(place, own, other):
    return (jnp.where(place == 0, own, other), jnp.where(place == 0, other, own))


def both(place, own, other):
    return jnp.concatenate(in_order(place, own, other), 0)


def spread_out(value, first, second):
    other = swap(value, first)
    pair = jnp.stack(in_order(lax.axis_index(first), value, other))
    return pair, swap(pair, second)


def placed(pair, other, second):
    pairs = in_order(lax.axis_index(second), pair, other)
    grid = jnp.stack(pairs, 0 if second == "y" else 1)
    return grid.reshape(-1, *grid.shape[3:])


def pick(array, axis, at):
    return lax.dynamic_index_in_dim(array, at, axis, keepdims=False)


def halve(value, axis, along=0):
    at = lax.axis_index(axis)
    return pick(value, along, at), swap(pick(value, along, 1 - at), axis)


def halve_x(value):
    return halve(value.reshape(2, 2, -1, value.shape[-1]), "x", 1)


def halve_y(value):
    return halve(value.reshape(2, 2, -1, value.shape[-1]), "y", 0)


def fast_body(
    tokens,
    positions,
    first_gain,
    query_weight,
    key_weight,
    value_weight,
    output_weight,
    second_gain,
    gate_weight,
    up_weight,
    down_weight,
    cotangent,
):
    seq = ("z", "c")
    fsdp = ("y", "x")
    z, core, half = lax.axis_index("z"), lax.axis_index("c"), lax.axis_index("x")
    near = z % 2
    lines = lax.axis_size("z")
    seq_count = 2 * lines
    shards = lax.axis_size("y") * 2
    spot = z * 2 + core
    quarter = near * 2 + core
    rows = tokens[0]
    count, width = rows.shape
    chip_count = 2 * count
    half_len = count * seq_count
    seq_len = 2 * half_len

    begins = jnp.where(
        (spot == 0) & (half == 0),
        count - 1 - positions[0, count - 1],
        half * half_len + spot * count - positions[0, 0],
    )
    ends = begins + (seq_len - count)
    scalars = jnp.stack([half, begins, ends, core]).astype(jnp.int32)

    gain_one = first_gain.astype(F32)[:, None]
    gain_two = second_gain.astype(F32)[:, None]

    def row_scale(value):
        return lax.rsqrt(jnp.mean(value * value, -1, keepdims=True) + EPS)

    take = functools.partial(lax.dynamic_slice_in_dim, axis=1)
    take_rows = functools.partial(lax.dynamic_slice_in_dim, axis=0)
    gather = lambda value, axes: lax.all_gather(value, axes, axis=0, tiled=True)
    own_rows = rows.astype(F32)
    own_unit_scale = row_scale(own_rows)
    own_unit = own_rows * own_unit_scale
    units = gather(own_unit.astype(LOW), seq)
    wide = QH // KVH * HD
    qkv_shard = (
        jnp.concatenate(
            [
                take(query_weight, spot * wide, wide),
                take(key_weight, spot * HD, HD),
                take(value_weight, spot * HD, HD),
            ],
            1,
        ).astype(F32)
        * gain_one
    ).astype(LOW)
    out_rows = output_weight.shape[0] // 2
    out_shard = take_rows(output_weight, core * out_rows, out_rows)
    piece = down_weight.shape[0] // 4
    down_shard = take_rows(down_weight, quarter * piece, piece)
    gate_shard, up_shard = (
        (
            jnp.concatenate(
                [
                    take(weight, shard * 4 * piece + quarter * piece, piece)
                    for shard in range(shards)
                ],
                1,
            ).astype(F32)
            * gain_two
        ).astype(LOW)
        for weight in (gate_weight, up_weight)
    )
    side = lax.axis_index("y")
    qkv_pair = jnp.stack(in_order(half, qkv_shard, swap(qkv_shard, "x")))
    gate_pair = jnp.stack(in_order(half, gate_shard, swap(gate_shard, "x")))
    up_pair = jnp.stack(in_order(side, up_shard, swap(up_shard, "y")))
    qkv_pair, gate_pair, up_pair = tie(qkv_pair, gate_pair, up_pair)
    qkv_w = placed(qkv_pair, swap(qkv_pair, "y"), "y")
    gate_pair, up_pair = (gate_pair, swap(gate_pair, "y")), (up_pair, swap(up_pair, "x"))

    place = half * half_len + jnp.arange(half_len, dtype=jnp.int32)
    start = jnp.where(place >= ends, ends, jnp.where(place >= begins, begins, 0))
    freq = THETA ** (-(jnp.arange(HD // 2, dtype=F32) * 2.0 / HD))
    angle = freq[:, None] * (place - start).astype(F32)[None, :]
    cosine, sine = jnp.cos(angle), jnp.sin(angle)
    chip_rows = both(core, rows, swap(rows, "c"))
    units, own_cot, chip_rows = tie(units, cotangent[0], chip_rows)
    own, leaving = spread(scalars, contract(qkv_w, units, 0, 1), cosine, sine)

    near_cot = swap_near(own_cot)
    other, out_shard, down_shard, near_cot, chip_cot, gate_pair, up_pair = tie(
        swap(leaving, "x"),
        out_shard,
        down_shard,
        near_cot,
        both(core, own_cot, swap(own_cot, "c")),
        gate_pair,
        up_pair,
    )
    out_w = gather(out_shard, fsdp)
    down_w = gather(down_shard, fsdp)
    near_other = swap(near_cot, "c")
    head_low, head_full, log_total = attend_forward(scalars, own, other, chip_count)
    exchange = lambda value: lax.all_to_all(
        value, ("z", "x"), split_axis=0, concat_axis=0, tiled=True
    )
    head_low, near_other = tie(head_low, near_other)
    lead_shard, tail_shard = pack(scalars, gain_one, query_weight, key_weight, value_weight)
    heads, gate_w, up_w, near_cot, lead_shard = tie(
        exchange(head_low),
        placed(*gate_pair, "y"),
        placed(*up_pair, "x"),
        jnp.concatenate([near_cot, near_other], 0),
        lead_shard,
    )
    lead_w = gather(lead_shard, fsdp)
    heads = heads.reshape(QH // 2 * HD, chip_count)

    mine_of = lambda value: take_rows(value, core * count, count)
    theirs_of = lambda value: take_rows(value, (1 - core) * count, count)
    branch = contract(heads, out_w, 0, 0).astype(LOW)
    middle = chip_rows.astype(F32) + (branch.astype(F32) + swap(branch, "c").astype(F32))
    middle_scale = row_scale(middle)
    chip_unit = middle * middle_scale
    own_middle, own_scale, own_middle_unit = (
        mine_of(middle),
        mine_of(middle_scale),
        mine_of(chip_unit),
    )
    chip_unit = chip_unit.astype(LOW)
    near_unit = swap_near(mine_of(chip_unit))

    def feed(unit):
        gate, upper = contract(unit, gate_w, 1, 0), contract(unit, up_w, 1, 0)
        sigma = jax.nn.sigmoid(gate)
        silu = gate * sigma
        return (silu * upper).astype(LOW), (gate, upper, sigma, silu)

    def feed_back(cot, kept):
        gate, upper, sigma, silu = kept
        grad_hidden = contract(cot, down_w, 1, 1)
        gate_low = (grad_hidden * upper * sigma * (1.0 + gate * (1.0 - sigma))).astype(LOW)
        upper_low = (grad_hidden * silu).astype(LOW)
        part = contract(gate_low, gate_w, 1, 1) + contract(upper_low, up_w, 1, 1)
        return gate_low, upper_low, part

    def chip_sum(chip_part, near_part):
        near_sum = near_part[:count].astype(F32) + swap(near_part[count:].astype(LOW), "c")
        own_sum = mine_of(chip_part).astype(F32) + swap(theirs_of(chip_part).astype(LOW), "c")
        return own_sum, near_sum.astype(LOW)

    stack = lambda first, second: jnp.concatenate([first, second], 0)
    scatter = lambda value: lax.psum_scatter(value, fsdp, scatter_dimension=0, tiled=True)
    chip_hidden, chip_kept = feed(chip_unit)
    near_unit, chip_hidden = tie(near_unit, chip_hidden)
    near_unit = jnp.concatenate([near_unit, swap(near_unit, "c")], 0)
    near_hidden, near_kept = feed(near_unit)
    down_part = contract(
        stack(chip_hidden, near_hidden), stack(chip_cot, near_cot), 0, 0
    ).astype(LOW)
    near_cot, down_part = tie(near_cot, down_part)
    near_gate, near_upper, near_part = feed_back(near_cot, near_kept)
    chip_gate, chip_upper, chip_part = feed_back(chip_cot, chip_kept)
    grad_two, near_sum = chip_sum(chip_part, near_part)

    def four(value, near_value):
        return value, swap(value, "c"), near_value, swap(near_value, "c")

    def halves_first(value):
        cut = value.shape[-1] // 2
        return halve_x(value[:, :cut]), halve_y(value[:, cut:])

    def halves_second(firsts):
        return halve(sum(firsts[0]), "y"), halve(sum(firsts[1]), "x")

    def halves_end(seconds):
        return jnp.concatenate([sum(seconds[0]), sum(seconds[1])], 1)

    down_first = halves_first(down_part)
    near_sum, near_gate, near_upper, chip_part = tie(
        near_sum, near_gate, near_upper, chip_part
    )
    grad_came = swap_near(near_sum)
    all_units = stack(chip_unit, near_unit)
    gate_part = contract(all_units, stack(chip_gate, near_gate), 0, 0).astype(LOW)
    up_part = contract(all_units, stack(chip_upper, near_upper), 0, 0).astype(LOW)
    feed_own, feed_near = chip_sum(
        contract(chip_hidden, down_w, 1, 0), contract(near_hidden, down_w, 1, 0)
    )
    gate_part, up_part, down_first, grad_came, feed_near = tie(
        gate_part, up_part, down_first, grad_came, feed_near
    )
    feed_near = swap_near(feed_near)
    down_second = halves_second(down_first)
    grad_two = grad_two + grad_came.astype(F32)
    grad_middle = own_cot.astype(F32) + own_scale * (
        grad_two - own_middle_unit * jnp.mean(grad_two * own_middle_unit, -1, keepdims=True)
    )
    own_branch, lead_w, down_second, gate_part, up_part = tie(
        grad_middle.astype(LOW), lead_w, down_second, gate_part, up_part
    )
    gate_grad, up_grad = scatter(gate_part), scatter(up_part)
    down_grad = halves_end(down_second)
    down_far = swap_far(down_grad)
    grad_branch = both(core, own_branch, swap(own_branch, "c"))
    grad_heads = contract(out_w, grad_branch, 1, 1).astype(LOW)
    grad_heads, grad_branch, down_far = tie(grad_heads, grad_branch, down_far)
    down_sum = down_grad + down_far
    output_part = contract(heads, grad_branch, 1, 0).astype(LOW)
    output_grad = scatter(output_part)
    grad_head, output_part, gate_grad, down_sum = tie(
        exchange(grad_heads.reshape(2 * lines, HD, chip_count)), output_part, gate_grad, down_sum
    )
    down_near = swap_near(down_sum)

    gate_far = swap_far(gate_grad)
    kept, leaving = attend_backward(scalars, own, other, grad_head, head_full, log_total)
    kept, leaving, gate_far, down_near, tail_shard, feed_near = tie(
        kept, leaving, gate_far, down_near, tail_shard, feed_near
    )
    tail_w = gather(tail_shard, fsdp)

    up_far = swap_far(up_grad)
    gate_sum = gate_grad + gate_far
    gate_near = swap_near(gate_sum)
    block_output = (own_middle + feed_own + feed_near.astype(F32)).astype(LOW)[None]
    came, up_far, gate_near, block_output, output_grad = tie(
        swap(leaving, "x"), up_far, gate_near, block_output, output_grad
    )

    qkv_low, by_line = merge(scalars, kept, came, cosine, sine, lines)
    token_grads = lax.all_to_all(by_line, "z", split_axis=0, concat_axis=0, tiled=True)
    qkv_part = contract(units, qkv_low, 0, 1).astype(LOW).reshape(shards, 2, -1, 4 * HD)
    qkv_first = halve_x(qkv_part[:, 0]), halve_y(qkv_part[:, 1])
    qkv_second = halves_second(qkv_first)
    qkv_grad = jnp.concatenate([sum(qkv_second[0]), sum(qkv_second[1])], 0)
    up_sum = up_grad + up_far
    up_near = swap_near(up_sum)
    down_pieces = four(down_sum, down_near)
    token_grads, qkv_grad, up_near, down_pieces = tie(
        token_grads, qkv_grad, up_near, down_pieces
    )
    all_qkv = gather(qkv_grad, seq)

    token_grads = token_grads.reshape(-1, chip_count)
    split = lead_w.shape[1]
    grad_one = contract(token_grads[:split], lead_w, 0, 1) + contract(
        token_grads[split:], tail_w, 0, 1
    )
    grad_one, output_came = tie(grad_one, swap_near(output_grad))
    output_sum = output_grad + output_came
    output_far = swap_far(output_sum)
    grad_one = mine_of(grad_one) + swap(theirs_of(grad_one).astype(LOW), "c").astype(F32)
    grad_rows = own_unit_scale * (
        grad_one - own_unit * jnp.mean(grad_one * own_unit, -1, keepdims=True)
    )
    input_grad = (grad_middle + grad_rows).astype(LOW)[None]

    order = jnp.stack([quarter, quarter ^ 1, quarter ^ 2, quarter ^ 3]).astype(jnp.int32)
    core_order = jnp.stack([core, 1 - core]).astype(jnp.int32)
    down_total = place_rows(order, down_pieces)
    gate_total, up_total, second_gain_grad = place_columns(
        order, gain_two, gate_weight, up_weight, four(gate_sum, gate_near), four(up_sum, up_near), shards
    )
    output_far, second_gain_grad, all_qkv = tie(output_far, second_gain_grad, all_qkv)
    output_own = output_sum + output_far
    output_total = place_rows(core_order, (output_own, swap(output_own, "c")))
    query_grad, key_grad, value_grad, first_gain_grad = place_heads(
        gain_one, query_weight, key_weight, value_weight, all_qkv
    )
    return (
        block_output,
        input_grad,
        first_gain_grad[:, 0],
        query_grad,
        key_grad,
        value_grad,
        output_total,
        second_gain_grad[:, 0],
        gate_total,
        up_total,
        down_total,
    )


def fast_solution(mesh):
    seq_count, shard_count = mesh.devices.shape
    fine = Mesh(
        mesh.devices.reshape(seq_count // 2, 2, shard_count // 2, 2), ("z", "c", "y", "x")
    )
    seq, fsdp = ("z", "c"), ("y", "x")
    matrix = P(fsdp, None)
    return jax.shard_map(
        fast_body,
        mesh=fine,
        in_specs=(
            P(fsdp, seq, None),
            P(fsdp, seq),
            P(fsdp),
            matrix,
            matrix,
            matrix,
            matrix,
            P(fsdp),
            matrix,
            matrix,
            matrix,
            P(fsdp, seq, None),
        ),
        out_specs=(
            P(fsdp, seq, None),
            P(fsdp, seq, None),
            P(fsdp),
            matrix,
            matrix,
            matrix,
            matrix,
            P(fsdp),
            matrix,
            matrix,
            matrix,
        ),
        check_vma=False,
    )


def solution(mesh):
    shape = dict(mesh.shape)
    if shape["seq"] == KVH and shape["fsdp"] == 4:
        return fast_solution(mesh)
    return plain_solution(mesh)


def shifted(value, axis, steps):
    count = lax.axis_size(axis)
    first, last = (max(0, -steps), min(count, count - steps))
    return lax.ppermute(value, axis, [(source, source + steps) for source in range(first, last)])


def rope_tables(position_rows):
    freq = THETA ** (-(jnp.arange(HD // 2, dtype=jnp.float32) * 2.0 / HD))
    angle = position_rows.astype(jnp.float32)[:, None] * freq[None, :]
    cosine = jnp.cos(angle)
    sine = jnp.sin(angle)
    return (jnp.concatenate([cosine, cosine], -1), jnp.concatenate([sine, sine], -1))


def rotate(values, cosine, sine):
    half = HD // 2
    turned = jnp.concatenate([-values[..., half:], values[..., :half]], -1)
    return values * cosine[:, None, :] + turned * sine[:, None, :]


def rotate_back(grads, cosine, sine):
    half = HD // 2
    scaled = grads * sine[:, None, :]
    turned = jnp.concatenate([scaled[..., half:], -scaled[..., :half]], -1)
    return grads * cosine[:, None, :] + turned


def norm_forward(rows, gain):
    scale = lax.rsqrt(jnp.mean(rows * rows, -1, keepdims=True) + EPS)
    unit = rows * scale
    return (unit * gain, unit, scale)


def norm_backward(grad_out, unit, scale, gain):
    grad_unit = grad_out * gain
    gain_grad = jnp.sum(grad_out * unit, 0)
    grad_rows = scale * (grad_unit - unit * jnp.mean(grad_unit * unit, -1, keepdims=True))
    return (grad_rows, gain_grad)


def plain_body(
    tokens,
    positions,
    first_gain,
    query_weight,
    key_weight,
    value_weight,
    output_weight,
    second_gain,
    gate_weight,
    up_weight,
    down_weight,
    cotangent,
):
    seq_count = lax.axis_size("seq")
    local_rows = tokens[0]
    token_count = local_rows.shape[0]
    half_len = token_count * seq_count
    rows_float = local_rows.astype(jnp.float32)
    gain_one, wq_full, wk_full, wv_full, wo_full = (
        lax.all_gather(first_gain, "fsdp", axis=0, tiled=True),
        lax.all_gather(query_weight, "fsdp", axis=0, tiled=True),
        lax.all_gather(key_weight, "fsdp", axis=0, tiled=True),
        lax.all_gather(value_weight, "fsdp", axis=0, tiled=True),
        lax.all_gather(output_weight, "fsdp", axis=0, tiled=True),
    )
    gain_one = gain_one.astype(jnp.float32)
    normed_one, unit_one, scale_one = norm_forward(rows_float, gain_one)
    normed_low = normed_one.astype(jnp.bfloat16)
    cosine, sine = rope_tables(positions[0])
    query_lin = jnp.dot(normed_low, wq_full, preferred_element_type=jnp.float32).reshape(
        token_count, QH, HD
    )
    key_lin = jnp.dot(normed_low, wk_full, preferred_element_type=jnp.float32).reshape(
        token_count, KVH, HD
    )
    value_lin = jnp.dot(normed_low, wv_full, preferred_element_type=jnp.float32).reshape(
        token_count, KVH, HD
    )
    query_rows = rotate(query_lin, cosine, sine).astype(jnp.bfloat16)
    key_rows = rotate(key_lin, cosine, sine).astype(jnp.bfloat16)
    value_rows = value_lin.astype(jnp.bfloat16)
    repeat = max(1, seq_count // KVH)
    if repeat > 1:
        key_rows = jnp.repeat(key_rows, repeat, axis=1)
        value_rows = jnp.repeat(value_rows, repeat, axis=1)
    query_heads, key_heads, value_heads = (
        lax.all_to_all(query_rows, "seq", split_axis=1, concat_axis=0, tiled=True),
        lax.all_to_all(key_rows, "seq", split_axis=1, concat_axis=0, tiled=True),
        lax.all_to_all(value_rows, "seq", split_axis=1, concat_axis=0, tiled=True),
    )
    head_count = query_heads.shape[1]
    pair_count = key_heads.shape[1]
    group = head_count // pair_count
    half_positions = lax.all_gather(positions[0], "seq", axis=0, tiled=True)
    key_prior, value_prior = shifted((key_heads, value_heads), "fsdp", 1)
    key_all = jnp.concatenate([key_prior, key_heads], 0)
    value_all = jnp.concatenate([value_prior, value_heads], 0)
    half_index = lax.axis_index("fsdp") % 2
    key_index = (half_index - 1) * half_len + jnp.arange(2 * half_len, dtype=jnp.int32)
    row_index = half_index * half_len + jnp.arange(half_len, dtype=jnp.int32)
    row_start = row_index - half_positions
    block = min(512, half_len)
    count = half_len // block
    factor = HD ** (-0.5)
    query_blocks = query_heads.reshape(count, block, pair_count, group, HD)
    index_blocks = row_index.reshape(count, block)
    start_blocks = row_start.reshape(count, block)

    def block_scores(query_block, index_block, start_block):
        scores = (
            jnp.einsum("bkgd,tkd->kgbt", query_block, key_all, preferred_element_type=jnp.float32)
            * factor
        )
        visible = (key_index[None, :] >= start_block[:, None]) & (
            key_index[None, :] <= index_block[:, None]
        )
        return jnp.where(visible, scores, -1e30)

    def forward_block(items):
        query_block, index_block, start_block = items
        scores = block_scores(query_block, index_block, start_block)
        top = jnp.max(scores, -1, keepdims=True)
        expo = jnp.exp(scores - top)
        total = jnp.sum(expo, -1, keepdims=True)
        probs_low = (expo / total).astype(jnp.bfloat16)
        mixed = jnp.einsum(
            "kgbt,tkd->bkgd", probs_low, value_all, preferred_element_type=jnp.float32
        )
        return (mixed.reshape(block, head_count, HD).astype(jnp.bfloat16), top + jnp.log(total))

    head_blocks, log_totals = lax.map(forward_block, (query_blocks, index_blocks, start_blocks))
    head_out = head_blocks.reshape(half_len, head_count, HD)
    token_heads = lax.all_to_all(head_out, "seq", split_axis=0, concat_axis=1, tiled=True)
    heads_flat = token_heads.reshape(token_count, QH * HD)
    middle = rows_float + jnp.dot(heads_flat, wo_full, preferred_element_type=jnp.float32)
    gain_two, wg_full, wu_full, wd_full = (
        lax.all_gather(second_gain, "fsdp", axis=0, tiled=True),
        lax.all_gather(gate_weight, "fsdp", axis=0, tiled=True),
        lax.all_gather(up_weight, "fsdp", axis=0, tiled=True),
        lax.all_gather(down_weight, "fsdp", axis=0, tiled=True),
    )
    gain_two = gain_two.astype(jnp.float32)
    normed_two, unit_two, scale_two = norm_forward(middle, gain_two)
    normed_two_low = normed_two.astype(jnp.bfloat16)
    gate = jnp.dot(normed_two_low, wg_full, preferred_element_type=jnp.float32)
    upper = jnp.dot(normed_two_low, wu_full, preferred_element_type=jnp.float32)
    hidden = (jax.nn.silu(gate) * upper).astype(jnp.bfloat16)
    result = middle + jnp.dot(hidden, wd_full, preferred_element_type=jnp.float32)
    block_output = result.astype(jnp.bfloat16)[None]
    grad_low = cotangent[0]
    grad_rows = grad_low.astype(jnp.float32)
    down_grad = jnp.einsum("tf,td->fd", hidden, grad_low, preferred_element_type=jnp.float32)
    grad_hidden = jnp.einsum("td,fd->tf", grad_low, wd_full, preferred_element_type=jnp.float32)
    sigma = jax.nn.sigmoid(gate)
    gate_low = (grad_hidden * upper * sigma * (1.0 + gate * (1.0 - sigma))).astype(jnp.bfloat16)
    upper_low = (grad_hidden * gate * sigma).astype(jnp.bfloat16)
    gate_grad = jnp.einsum(
        "td,tf->df", normed_two_low, gate_low, preferred_element_type=jnp.float32
    )
    up_grad = jnp.einsum("td,tf->df", normed_two_low, upper_low, preferred_element_type=jnp.float32)
    grad_normed_two = jnp.einsum(
        "tf,df->td", gate_low, wg_full, preferred_element_type=jnp.float32
    ) + jnp.einsum("tf,df->td", upper_low, wu_full, preferred_element_type=jnp.float32)
    grad_middle_norm, second_gain_grad = norm_backward(
        grad_normed_two, unit_two, scale_two, gain_two
    )
    grad_middle = grad_rows + grad_middle_norm
    grad_branch = grad_middle.astype(jnp.bfloat16)
    output_grad = jnp.einsum(
        "tc,td->cd", heads_flat, grad_branch, preferred_element_type=jnp.float32
    )
    grad_heads = (
        jnp.einsum("td,cd->tc", grad_branch, wo_full, preferred_element_type=jnp.float32)
        .astype(jnp.bfloat16)
        .reshape(token_count, QH, HD)
    )
    grad_head_rows = lax.all_to_all(grad_heads, "seq", split_axis=1, concat_axis=0, tiled=True)
    grad_blocks = grad_head_rows.reshape(count, block, pair_count, group, HD)

    def backward_block(carry, items):
        key_acc, value_acc = carry
        query_block, index_block, start_block, grad_block, log_block = items
        scores = block_scores(query_block, index_block, start_block)
        probs = jnp.exp(scores - log_block)
        probs_low = probs.astype(jnp.bfloat16)
        grad_probs = jnp.einsum(
            "bkgd,tkd->kgbt", grad_block, value_all, preferred_element_type=jnp.float32
        )
        grad_scores = (
            probs * (grad_probs - jnp.sum(probs * grad_probs, -1, keepdims=True))
        ).astype(jnp.bfloat16)
        query_grad_block = (
            jnp.einsum("kgbt,tkd->bkgd", grad_scores, key_all, preferred_element_type=jnp.float32)
            * factor
        )
        key_acc = (
            key_acc
            + jnp.einsum(
                "kgbt,bkgd->tkd", grad_scores, query_block, preferred_element_type=jnp.float32
            )
            * factor
        )
        value_acc = value_acc + jnp.einsum(
            "kgbt,bkgd->tkd", probs_low, grad_block, preferred_element_type=jnp.float32
        )
        return ((key_acc, value_acc), query_grad_block.reshape(block, head_count, HD))

    empty = jnp.zeros((2 * half_len, pair_count, HD), jnp.float32)
    (key_acc, value_acc), query_grad_blocks = lax.scan(
        backward_block,
        (empty, empty),
        (query_blocks, index_blocks, start_blocks, grad_blocks, log_totals),
    )
    key_back, value_back = (
        shifted(key_acc[:half_len].astype(jnp.bfloat16), "fsdp", -1).astype(jnp.float32),
        shifted(value_acc[:half_len].astype(jnp.bfloat16), "fsdp", -1).astype(jnp.float32),
    )
    key_local = key_acc[half_len:] + key_back
    value_local = value_acc[half_len:] + value_back
    query_grad_heads = query_grad_blocks.reshape(half_len, head_count, HD)
    grad_query_tok, grad_key_tok, grad_value_tok = (
        lax.all_to_all(
            query_grad_heads.astype(jnp.bfloat16), "seq", split_axis=0, concat_axis=1, tiled=True
        ).astype(query_grad_heads.dtype),
        lax.all_to_all(
            key_local.astype(jnp.bfloat16), "seq", split_axis=0, concat_axis=1, tiled=True
        ).astype(key_local.dtype),
        lax.all_to_all(
            value_local.astype(jnp.bfloat16), "seq", split_axis=0, concat_axis=1, tiled=True
        ).astype(value_local.dtype),
    )
    if repeat > 1:
        grad_key_tok = grad_key_tok.reshape(token_count, KVH, repeat, HD).sum(2)
        grad_value_tok = grad_value_tok.reshape(token_count, KVH, repeat, HD).sum(2)
    query_lin_grad = (
        rotate_back(grad_query_tok, cosine, sine).astype(jnp.bfloat16).reshape(token_count, QH * HD)
    )
    key_lin_grad = (
        rotate_back(grad_key_tok, cosine, sine).astype(jnp.bfloat16).reshape(token_count, KVH * HD)
    )
    value_lin_grad = grad_value_tok.astype(jnp.bfloat16).reshape(token_count, KVH * HD)
    query_grad = jnp.einsum(
        "td,tc->dc", normed_low, query_lin_grad, preferred_element_type=jnp.float32
    )
    key_grad = jnp.einsum("td,tc->dc", normed_low, key_lin_grad, preferred_element_type=jnp.float32)
    value_grad = jnp.einsum(
        "td,tc->dc", normed_low, value_lin_grad, preferred_element_type=jnp.float32
    )
    grad_normed_one = jnp.einsum(
        "tc,dc->td", query_lin_grad, wq_full, preferred_element_type=jnp.float32
    )
    grad_normed_one = grad_normed_one + jnp.einsum(
        "tc,dc->td", key_lin_grad, wk_full, preferred_element_type=jnp.float32
    )
    grad_normed_one = grad_normed_one + jnp.einsum(
        "tc,dc->td", value_lin_grad, wv_full, preferred_element_type=jnp.float32
    )
    grad_rows_one, first_gain_grad = norm_backward(grad_normed_one, unit_one, scale_one, gain_one)
    input_grad = (grad_middle + grad_rows_one).astype(jnp.bfloat16)[None]
    pieces = (
        lax.psum_scatter(
            first_gain_grad.astype(jnp.bfloat16), "fsdp", scatter_dimension=0, tiled=True
        ).astype(jnp.float32),
        lax.psum_scatter(
            query_grad.astype(jnp.bfloat16), "fsdp", scatter_dimension=0, tiled=True
        ).astype(jnp.float32),
        lax.psum_scatter(
            key_grad.astype(jnp.bfloat16), "fsdp", scatter_dimension=0, tiled=True
        ).astype(jnp.float32),
        lax.psum_scatter(
            value_grad.astype(jnp.bfloat16), "fsdp", scatter_dimension=0, tiled=True
        ).astype(jnp.float32),
        lax.psum_scatter(
            output_grad.astype(jnp.bfloat16), "fsdp", scatter_dimension=0, tiled=True
        ).astype(jnp.float32),
        lax.psum_scatter(
            second_gain_grad.astype(jnp.bfloat16), "fsdp", scatter_dimension=0, tiled=True
        ).astype(jnp.float32),
        lax.psum_scatter(
            gate_grad.astype(jnp.bfloat16), "fsdp", scatter_dimension=0, tiled=True
        ).astype(jnp.float32),
        lax.psum_scatter(
            up_grad.astype(jnp.bfloat16), "fsdp", scatter_dimension=0, tiled=True
        ).astype(jnp.float32),
        lax.psum_scatter(
            down_grad.astype(jnp.bfloat16), "fsdp", scatter_dimension=0, tiled=True
        ).astype(jnp.float32),
    )
    shares = (
        lax.psum(pieces[0].astype(jnp.bfloat16), "seq").astype(jnp.float32),
        lax.psum(pieces[1].astype(jnp.bfloat16), "seq").astype(jnp.float32),
        lax.psum(pieces[2].astype(jnp.bfloat16), "seq").astype(jnp.float32),
        lax.psum(pieces[3].astype(jnp.bfloat16), "seq").astype(jnp.float32),
        lax.psum(pieces[4].astype(jnp.bfloat16), "seq").astype(jnp.float32),
        lax.psum(pieces[5].astype(jnp.bfloat16), "seq").astype(jnp.float32),
        lax.psum(pieces[6].astype(jnp.bfloat16), "seq").astype(jnp.float32),
        lax.psum(pieces[7].astype(jnp.bfloat16), "seq").astype(jnp.float32),
        lax.psum(pieces[8].astype(jnp.bfloat16), "seq").astype(jnp.float32),
    )
    return (
        block_output,
        input_grad,
        shares[0],
        shares[1],
        shares[2],
        shares[3],
        shares[4],
        shares[5],
        shares[6],
        shares[7],
        shares[8],
    )


def plain_solution(mesh):
    placed = (
        P("fsdp", "seq", None),
        P("fsdp", "seq"),
        P("fsdp"),
        P("fsdp", None),
        P("fsdp", None),
        P("fsdp", None),
        P("fsdp", None),
        P("fsdp"),
        P("fsdp", None),
        P("fsdp", None),
        P("fsdp", None),
        P("fsdp", "seq", None),
    )
    return jax.shard_map(
        plain_body,
        mesh=mesh,
        in_specs=placed,
        out_specs=(
            P("fsdp", "seq", None),
            P("fsdp", "seq", None),
            P("fsdp"),
            P("fsdp", None),
            P("fsdp", None),
            P("fsdp", None),
            P("fsdp", None),
            P("fsdp"),
            P("fsdp", None),
            P("fsdp", None),
            P("fsdp", None),
        ),
        check_vma=False,
    )
```

profile of v0, /device:TPU:0, one launch (start us, length us, event | category | flops | bytes accessed | tf_op | source)
XLA Modules:
  0.0 569.3 jit_solution(8552843462291538722)
XLA Ops:
  27.8 13.6 %collective-permute-done.1 = bf16[384,1024]{1,0:T(8,128)(2,1)} collective-permute-done((bf16[384,1024]{1,0:T(8,128)(2,1)}, bf16[384,1024]{1,0:T(8,128)(2,1)}, u32[]{:S(2)}, u32[]{:S(2)}) %collective-permute-start.1) | collective-permute-done | bytes 786464 | tf_op jit(solution)/shard_map/ppermute | solution.py:540
  53.5 9.7 %collective-permute-done.3 = bf16[2,384,384]{2,1,0:T(8,128)(2,1)S(1)} collective-permute-done((bf16[2,384,384]{2,1,0:T(8,128)(2,1)S(1)}, bf16[2,384,384]{2,1,0:T(8,128)(2,1)S(1)}, u32[]{:S(2)}, u32[]{:S(2)}) %collective-permute-start.3) | collective-permute-done | bytes 589856 | tf_op jit(solution)/shard_map/ppermute | solution.py:540
  64.5 14.1 %all-gather.7.cloned.1.call-done = bf16[2048,1536]{1,0:T(8,128)(2,1)} async-done(((bf16[256,1536]{1,0:T(8,128)(2,1)}), bf16[2048,1536]{1,0:T(8,128)(2,1)}) %all-gather.7.cloned.1.call-update) | async-done | bytes 6291472 | tf_op jit(solution)/shard_map/all_gather | solution.py:637
  95.3 15.6 %collective-permute-done.6 = bf16[256,1536]{1,0:T(8,128)(2,1)} collective-permute-done((bf16[256,1536]{1,0:T(8,128)(2,1)}, bf16[256,1536]{1,0:T(8,128)(2,1)}, u32[]{:S(2)}, u32[]{:S(2)}) %collective-permute-start.6) | collective-permute-done | bytes 786464 | tf_op jit(solution)/shard_map/ppermute | solution.py:544
  110.9 5.4 collective-permute-done.5.other_ref
  121.6 26.2 %attend_forward.1 = (bf16[8,96,512]{2,1,0:T(8,128)(2,1)S(1)}, f32[8,96,512]{2,1,0:T(8,128)S(1)}, f32[8,1,512]{2,1,0:T(1,128)S(1)}) custom-call(s32[4]{0:T(128)S(1)} %pad_add_fusion.scalars, bf16[288,2048]{1,0:T(8,128)(2,1)S(1)} %copy-done.34, bf16[288,2048]{1,0:T(8,128)(2,1)} %collective-permute-done.5.other_ref), custom_call_target="tpu_custom_call" | custom-call | flops 28991029248 | bytes 10485760 | tf_op jit(solution)/shard_map/attend_forward/pallas_call | solution.py:200
  164.3 8.9 %all-to-all-done = bf16[8,96,512]{2,1,0:T(8,128)(2,1)} async-done(((bf16[8,96,512]{2,1,0:T(8,128)(2,1)}), bf16[8,96,512]{2,1,0:T(8,128)(2,1)}, u32[]{:S(2)}, u32[]{:S(2)}) %all-to-all-start) | async-done | bytes 786464 | tf_op jit(solution)/shard_map/all_to_all | solution.py:702
  195.2 5.6 all-gather.11.cloned.1.call-done
  200.8 6.2 %multiply_convert_fusion.4 = (bf16[512,1024]{1,0:T(8,128)(2,1)S(1)}, bf16[512,1024]{1,0:T(8,128)(2,1)S(1)}, bf16[512,1024]{1,0:T(8,128)(2,1)S(1)}) fusion(f32[512,1024]{1,0:T(8,128)} %fusion.41, f32[512,1024]{1,0:T(8,128)} %fusion.40, bf16[512,1536]{1,0:T(8,128)(2,1)} %pad_maximum_fusion.6, bf16[1024,1536]{1,0:T(8,128)(2,1)} %all-gather.11.cloned.1.call-done), kind=kOutput, calls=%fused_computation.32 | convolution fusion | flops 1618477056 | bytes 12058624 | tf_op jit(solution)/shard_map/dot_general | solution.py:26
  239.1 6.3 %convolution_convert_fusion.1 = bf16[1536,1024]{1,0:T(8,128)(2,1)} fusion(bf16[512,1024]{1,0:T(8,128)(2,1)S(1)} %get-tuple-element.131, bf16[512,1024]{1,0:T(8,128)(2,1)S(1)} %get-tuple-element.202, bf16[256,1536]{1,0:T(8,128)(2,1)S(1)} %collective-permute-done.14, bf16[256,1536]{1,0:T(8,128)(2,1)} %collective-permute-done.13, ...), kind=kOutput, calls=%fused_computation.1 | convolution fusion | flops 3236429824 | bytes 8388608 | tf_op jit(solution)/shard_map/dot_general | solution.py:26
  245.3 7.4 %convolution_convert_fusion = bf16[1536,1024]{1,0:T(8,128)(2,1)} fusion(bf16[512,1024]{1,0:T(8,128)(2,1)} %copy-done.82, bf16[512,1024]{1,0:T(8,128)(2,1)} %copy-done.81, bf16[256,1536]{1,0:T(8,128)(2,1)} %copy-done.65, bf16[256,1536]{1,0:T(8,128)(2,1)} %collective-permute-done.13, bf16[512,1536]{1,0:T(8,128)(2,1)S(1)} %copy-done.48), kind=kOutput, calls=%fused_computation | convolution fusion | flops 3236429824 | bytes 8388608 | tf_op jit(solution)/shard_map/dot_general | solution.py:26
  285.3 29.1 %collective-permute-done.23 = bf16[256,1536]{1,0:T(8,128)(2,1)S(1)} collective-permute-done((bf16[256,1536]{1,0:T(8,128)(2,1)S(1)}, bf16[256,1536]{1,0:T(8,128)(2,1)S(1)}, u32[]{:S(2)}, u32[]{:S(2)}) %collective-permute-start.23) | collective-permute-done | bytes 786464 | tf_op jit(solution)/shard_map/ppermute | solution.py:548
  332.6 7.9 %all-to-all-done.1.grad_ref = bf16[8,96,512]{2,1,0:T(8,128)(2,1)S(1)} async-done(((bf16[8,96,512]{2,1,0:T(8,128)(2,1)}), bf16[8,96,512]{2,1,0:T(8,128)(2,1)S(1)}, u32[]{:S(2)}, u32[]{:S(2)}) %all-to-all-start.1) | async-done | bytes 786464 | tf_op jit(solution)/shard_map/all_to_all | solution.py:702
  345.6 33.9 %attend_backward.1 = (bf16[288,2048]{1,0:T(8,128)(2,1)S(1)}, bf16[288,2048]{1,0:T(8,128)(2,1)S(1)}) custom-call(s32[4]{0:T(128)S(1)} %pad_add_fusion.scalars, bf16[288,2048]{1,0:T(8,128)(2,1)S(1)} %copy-done.34, bf16[288,2048]{1,0:T(8,128)(2,1)} %collective-permute-done.5.other_ref, bf16[8,96,512]{2,1,0:T(8,128)(2,1)S(1)} %copy-done.29, ...), custom_call_target="tpu_custom_call" | custom-call | flops 38050725888 | bytes 16777216 | tf_op jit(solution)/shard_map/attend_backward/pallas_call | solution.py:244
  381.5 5.8 %collective-permute-done.25.refs_2_ = bf16[256,1536]{1,0:T(8,128)(2,1)} collective-permute-done((bf16[256,1536]{1,0:T(8,128)(2,1)}, bf16[256,1536]{1,0:T(8,128)(2,1)}, u32[]{:S(2)}, u32[]{:S(2)}) %collective-permute-start.25) | collective-permute-done | bytes 786464 | tf_op jit(solution)/shard_map/ppermute | solution.py:544
  397.5 20.5 %reduce-scatter.8.cloned.1.call-done = bf16[192,1536]{1,0:T(8,128)(2,1)} async-done(((bf16[768,1536]{1,0:T(8,128)(2,1)}), bf16[192,1536]{1,0:T(8,128)(2,1)}) %reduce-scatter.8.cloned.1.call-update) | async-done | bytes 589840 | tf_op jit(solution)/shard_map/reduce_scatter | solution.py:751
  418.0 8.0 %collective-permute-done.28 = bf16[384,1024]{1,0:T(8,128)(2,1)S(1)} collective-permute-done((bf16[384,1024]{1,0:T(8,128)(2,1)}, bf16[384,1024]{1,0:T(8,128)(2,1)S(1)}, u32[]{:S(2)}, u32[]{:S(2)}) %collective-permute-start.28) | collective-permute-done | bytes 786464 | tf_op jit(solution)/shard_map/ppermute | solution.py:548
  439.4 6.3 %convolution_convert_fusion.5 = bf16[1536,384]{1,0:T(8,128)(2,1)S(1)} fusion(bf16[2048,1536]{1,0:T(8,128)(2,1)} %all-gather.7.cloned.1.call-done, bf16[384,2048]{1,0:T(8,128)(2,1)S(1)} %get-tuple-element.169), kind=kOutput, calls=%fused_computation.16 | convolution fusion | flops 2416508928 | bytes 9043968 | tf_op jit(solution)/shard_map/dot_general | solution.py:26
  451.7 9.7 %collective-permute-done.33 = bf16[2,192,384]{2,1,0:T(8,128)(2,1)S(1)} collective-permute-done((bf16[2,192,384]{2,1,0:T(8,128)(2,1)S(1)}, bf16[2,192,384]{2,1,0:T(8,128)(2,1)S(1)}, u32[]{:S(2)}, u32[]{:S(2)}) %collective-permute-start.33) | collective-permute-done | bytes 294944 | tf_op jit(solution)/shard_map/ppermute | solution.py:540
  469.8 13.1 %collective-permute-done.35.refs_6_ = bf16[384,1024]{1,0:T(8,128)(2,1)} collective-permute-done((bf16[384,1024]{1,0:T(8,128)(2,1)}, bf16[384,1024]{1,0:T(8,128)(2,1)}, u32[]{:S(2)}, u32[]{:S(2)}) %collective-permute-start.35) | collective-permute-done | bytes 786464 | tf_op jit(solution)/shard_map/ppermute | solution.py:544
  491.5 22.9 %collective-permute-done.38 = bf16[192,1536]{1,0:T(8,128)(2,1)} collective-permute-done((bf16[192,1536]{1,0:T(8,128)(2,1)}, bf16[192,1536]{1,0:T(8,128)(2,1)}, u32[]{:S(2)}, u32[]{:S(2)}) %collective-permute-start.38) | collective-permute-done | bytes 589856 | tf_op jit(solution)/shard_map/ppermute | solution.py:544
  521.5 6.4 %place_rows.3 = f32[1024,1536]{1,0:T(8,128)} custom-call(s32[4]{0:T(128)S(1)} %pad_add_fusion.1.order, bf16[256,1536]{1,0:T(8,128)(2,1)} %fusion.32.refs_0_, bf16[256,1536]{1,0:T(8,128)(2,1)S(1)} %copy-done.23, bf16[256,1536]{1,0:T(8,128)(2,1)} %collective-permute-done.25.refs_2_, bf16[256,1536]{1,0:T(8,128)(2,1)S(1)} %copy-done.25), custom_call_target="tpu_custom_call" | custom-call | bytes 9437184 | tf_op jit(solution)/shard_map/place_rows/pallas_call | solution.py:292
  527.9 9.4 %place_columns.1 = (f32[384,4096]{1,0:T(8,128)}, f32[384,4096]{1,0:T(8,128)}, f32[384,1]{1,0:T(8,128)S(1)}) custom-call(s32[4]{0:T(128)S(1)} %pad_add_fusion.1.order, f32[384,1]{1,0:T(8,128)S(1)} %broadcast_in_dim.31.gain_ref, bf16[384,4096]{1,0:T(8,128)(2,1)S(1)} %copy-done.5, bf16[384,4096]{1,0:T(8,128)(2,1)S(1)} %copy-done.4, ...), custom_call_target="tpu_custom_call" | custom-call | flops 9437184 | bytes 25165824 | tf_op jit(solution)/shard_map/place_columns/pallas_call | solution.py:338
  539.4 8.5 %collective-permute-done.40 = bf16[192,1536]{1,0:T(8,128)(2,1)} collective-permute-done((bf16[192,1536]{1,0:T(8,128)(2,1)}, bf16[192,1536]{1,0:T(8,128)(2,1)}, u32[]{:S(2)}, u32[]{:S(2)}) %collective-permute-start.40) | collective-permute-done | bytes 589856 | tf_op jit(solution)/shard_map/ppermute | solution.py:548
  (387 shorter events, 252.3 us)
Async XLA Ops:
  7.2 71.4 %all-gather.7.cloned.1.call-start = ((), (), s32[]{:S(2)}) async-start(), calls=%async_computation.6 | async-start | bytes 7077888 | tf_op jit(solution)/shard_map/all_gather | solution.py:637
  11.0 162.2 %all-gather.9.cloned.1.call-start = ((), (), s32[]{:S(2)}) async-start(), calls=%async_computation.7 | async-start | bytes 2949120 | tf_op jit(solution)/shard_map/all_gather | solution.py:637
  48.8 46.5 %collective-permute-start.8 = (bf16[2,384,1024]{2,1,0:T(8,128)(2,1)}, bf16[2,384,1024]{2,1,0:T(8,128)(2,1)}, u32[]{:S(2)}, u32[]{:S(2)}) collective-permute-start(bf16[2,384,1024]{2,1,0:T(8,128)(2,1)} %pad_maximum_fusion.3), channel_id=1, source_target_pairs={{0,2},{2,0},{1,3},{3,1},{4,6},{6,4},{5,7},{7,5},{8,10},{10,8},{9,1... | collective-permute-start | bytes 4718600 | tf_op jit(solution)/shard_map/ppermute | solution.py:540
  49.0 46.3 %collective-permute-start.9 = (bf16[2,384,1024]{2,1,0:T(8,128)(2,1)}, bf16[2,384,1024]{2,1,0:T(8,128)(2,1)}, u32[]{:S(2)}, u32[]{:S(2)}) collective-permute-start(bf16[2,384,1024]{2,1,0:T(8,128)(2,1)} %pad_maximum_fusion.4), channel_id=1, source_target_pairs={{0,1},{1,0},{2,3},{3,2},{4,5},{5,4},{6,7},{7,6},{8,9},{9,8},{10,11... | collective-permute-start | bytes 4718600 | tf_op jit(solution)/shard_map/ppermute | solution.py:540
  116.4 84.5 %all-gather.11.cloned.1.call-start = ((), (), s32[]{:S(2)}) async-start(), calls=%async_computation.8 | async-start | bytes 3932160 | tf_op jit(solution)/shard_map/all_gather | solution.py:637
  152.9 117.1 %all-gather.13.cloned.1.call-start = ((), (), s32[]{:S(2)}) async-start(), calls=%async_computation.9 | async-start | bytes 2949120 | tf_op jit(solution)/shard_map/all_gather | solution.py:637
  177.9 163.4 %reduce-scatter.4.cloned.1.call-start = ((), (), s32[]{:S(2)}) async-start(), calls=%async_computation.10 | async-start | bytes 3932160 | tf_op jit(solution)/shard_map/reduce_scatter | solution.py:751
  213.0 51.9 %collective-permute-start.12 = (bf16[256,1536]{1,0:T(8,128)(2,1)}, bf16[256,1536]{1,0:T(8,128)(2,1)}, u32[]{:S(2)}, u32[]{:S(2)}) collective-permute-start(bf16[256,1536]{1,0:T(8,128)(2,1)} %dynamic-slice_convert_fusion.2), channel_id=1, source_target_pairs={{0,4},{4,0},{1,5},{5,1},{2,6},{6,2},{3,7},{7,3},{8,12},{12,8},{9,1... | collective-permute-start | bytes 2359304 | tf_op jit(solution)/shard_map/ppermute | solution.py:540
  274.7 114.2 %reduce-scatter.6.cloned.1.call-start = ((), (), s32[]{:S(2)}) async-start(), calls=%async_computation.11 | async-start | bytes 3932160 | tf_op jit(solution)/shard_map/reduce_scatter | solution.py:751
  276.9 37.4 %collective-permute-start.23 = (bf16[256,1536]{1,0:T(8,128)(2,1)S(1)}, bf16[256,1536]{1,0:T(8,128)(2,1)S(1)}, u32[]{:S(2)}, u32[]{:S(2)}) collective-permute-start(bf16[256,1536]{1,0:T(8,128)(2,1)S(1)} %pad_maximum_fusion.12), channel_id=1, source_target_pairs={{0,16},{16,0},{8,24},{24,8},{1,17},{17,1},{9,25},{25,9},{2,18},{18... | collective-permute-start | bytes 2359304 | tf_op jit(solution)/shard_map/ppermute | solution.py:548
  319.9 98.1 %reduce-scatter.8.cloned.1.call-start = ((), (), s32[]{:S(2)}) async-start(), calls=%async_computation.12 | async-start | bytes 2949120 | tf_op jit(solution)/shard_map/reduce_scatter | solution.py:751
  324.5 162.0 %all-gather.15.cloned.1.call-start = ((), (), s32[]{:S(2)}) async-start(), calls=%async_computation.13 | async-start | bytes 2949120 | tf_op jit(solution)/shard_map/all_gather | solution.py:637
  329.5 64.3 %collective-permute-start.30 = (bf16[256,1536]{1,0:T(8,128)(2,1)}, bf16[256,1536]{1,0:T(8,128)(2,1)}, u32[]{:S(2)}, u32[]{:S(2)}) collective-permute-start(bf16[256,1536]{1,0:T(8,128)(2,1)} %dynamic-slice_convert_fusion.1), channel_id=1, source_target_pairs={{0,4},{4,0},{1,5},{5,1},{2,6},{6,2},{3,7},{7,3},{8,12},{12,8},{9,1... | collective-permute-start | bytes 2359304 | tf_op jit(solution)/shard_map/ppermute | solution.py:540
  329.5 52.0 %collective-permute-start.26 = (bf16[256,1536]{1,0:T(8,128)(2,1)}, bf16[256,1536]{1,0:T(8,128)(2,1)}, u32[]{:S(2)}, u32[]{:S(2)}) collective-permute-start(bf16[256,1536]{1,0:T(8,128)(2,1)} %fusion.23), channel_id=1, source_target_pairs={{0,8},{8,0},{16,24},{24,16},{1,9},{9,1},{17,25},{25,17},{2,10},{10... | collective-permute-start | bytes 2359304 | tf_op jit(solution)/shard_map/ppermute | solution.py:544
  341.3 40.2 %collective-permute-start.24 = (bf16[384,1024]{1,0:T(8,128)(2,1)}, bf16[384,1024]{1,0:T(8,128)(2,1)}, u32[]{:S(2)}, u32[]{:S(2)}) collective-permute-start(bf16[384,1024]{1,0:T(8,128)(2,1)} %reduce-scatter.4.cloned.1.call-done), channel_id=1, source_target_pairs={{0,16},{16,0},{8,24},{24,8},{1,17},{17,1},{9,25},{25,9},{2,18},{18... | collective-permute-start | bytes 2359304 | tf_op jit(solution)/shard_map/ppermute | solution.py:548
  341.3 46.0 %collective-permute-start.25 = (bf16[256,1536]{1,0:T(8,128)(2,1)}, bf16[256,1536]{1,0:T(8,128)(2,1)}, u32[]{:S(2)}, u32[]{:S(2)}) collective-permute-start(bf16[256,1536]{1,0:T(8,128)(2,1)} %fusion.32.refs_0_), channel_id=1, source_target_pairs={{0,8},{8,0},{16,24},{24,16},{1,9},{9,1},{17,25},{25,17},{2,10},{10... | collective-permute-start | bytes 2359304 | tf_op jit(solution)/shard_map/ppermute | solution.py:544
  387.4 40.3 %collective-permute-start.27 = (bf16[288,2048]{1,0:T(8,128)(2,1)}, bf16[288,2048]{1,0:T(8,128)(2,1)S(1)}, u32[]{:S(2)}, u32[]{:S(2)}) collective-permute-start(bf16[288,2048]{1,0:T(8,128)(2,1)} %copy-done.35), channel_id=1, source_target_pairs={{0,1},{1,0},{2,3},{3,2},{4,5},{5,4},{6,7},{7,6},{8,9},{9,8},{10,11... | collective-permute-start | bytes 3538952 | tf_op jit(solution)/shard_map/ppermute | solution.py:540
  388.9 37.1 %collective-permute-start.28 = (bf16[384,1024]{1,0:T(8,128)(2,1)}, bf16[384,1024]{1,0:T(8,128)(2,1)S(1)}, u32[]{:S(2)}, u32[]{:S(2)}) collective-permute-start(bf16[384,1024]{1,0:T(8,128)(2,1)} %reduce-scatter.6.cloned.1.call-done), channel_id=1, source_target_pairs={{0,16},{16,0},{8,24},{24,8},{1,17},{17,1},{9,25},{25,9},{2,18},{18... | collective-permute-start | bytes 2359304 | tf_op jit(solution)/shard_map/ppermute | solution.py:548
  391.5 36.2 %collective-permute-start.29 = (bf16[384,1024]{1,0:T(8,128)(2,1)S(1)}, bf16[384,1024]{1,0:T(8,128)(2,1)}, u32[]{:S(2)}, u32[]{:S(2)}) collective-permute-start(bf16[384,1024]{1,0:T(8,128)(2,1)S(1)} %add.291.refs_0_), channel_id=1, source_target_pairs={{0,8},{8,0},{16,24},{24,16},{1,9},{9,1},{17,25},{25,17},{2,10},{10... | collective-permute-start | bytes 2359304 | tf_op jit(solution)/shard_map/ppermute | solution.py:544
  434.6 48.3 %all-to-all-start.2 = ((bf16[4,384,512]{2,1,0:T(8,128)(2,1)}), bf16[4,384,512]{2,1,0:T(8,128)(2,1)}, u32[]{:S(2)}, u32[]{:S(2)}) async-start(bf16[4,384,512]{2,1,0:T(8,128)(2,1)} %get-tuple-element.168), calls=%async_computation.5 | async-start | bytes 3145728 | tf_op jit(solution)/shard_map/all_to_all | solution.py:830
  438.9 108.9 %all-gather.17.cloned.1.call-start = ((), (), s32[]{:S(2)}) async-start(), calls=%async_computation.14 | async-start | bytes 2654208 | tf_op jit(solution)/shard_map/all_gather | solution.py:637
  482.9 35.0 %collective-permute-start.41 = (bf16[384,1024]{1,0:T(8,128)(2,1)S(1)}, bf16[384,1024]{1,0:T(8,128)(2,1)S(1)}, u32[]{:S(2)}, u32[]{:S(2)}) collective-permute-start(bf16[384,1024]{1,0:T(8,128)(2,1)S(1)} %copy-done.9), channel_id=1, source_target_pairs={{0,4},{4,0},{1,5},{5,1},{2,6},{6,2},{3,7},{7,3},{8,12},{12,8},{9,1... | collective-permute-start | bytes 2359304 | tf_op jit(solution)/shard_map/ppermute | solution.py:540
  483.0 44.9 %collective-permute-start.43 = (bf16[384,1024]{1,0:T(8,128)(2,1)}, bf16[384,1024]{1,0:T(8,128)(2,1)}, u32[]{:S(2)}, u32[]{:S(2)}) collective-permute-start(bf16[384,1024]{1,0:T(8,128)(2,1)} %add.299.refs_4_), channel_id=1, source_target_pairs={{0,4},{4,0},{1,5},{5,1},{2,6},{6,2},{3,7},{7,3},{8,12},{12,8},{9,1... | collective-permute-start | bytes 2359304 | tf_op jit(solution)/shard_map/ppermute | solution.py:540
  483.8 44.0 %collective-permute-start.42 = (bf16[384,1024]{1,0:T(8,128)(2,1)}, bf16[384,1024]{1,0:T(8,128)(2,1)}, u32[]{:S(2)}, u32[]{:S(2)}) collective-permute-start(bf16[384,1024]{1,0:T(8,128)(2,1)} %collective-permute-done.29.refs_2_), channel_id=1, source_target_pairs={{0,4},{4,0},{1,5},{5,1},{2,6},{6,2},{3,7},{7,3},{8,12},{12,8},{9,1... | collective-permute-start | bytes 2359304 | tf_op jit(solution)/shard_map/ppermute | solution.py:540
  (117 other events, 1226.3 us)
Sparse Core Ops, SparseCore 0:
  11.2 67.4 all-gather.6
  116.5 36.2 all-gather.8
  155.2 45.6 all-gather.10
  202.5 43.8 all-gather.12
  274.8 43.9 reduce-scatter.3
  321.6 46.2 reduce-scatter.5
  371.5 46.4 reduce-scatter.7
  419.9 43.9 all-gather.14
  483.0 36.4 all-gather.16
where the time goes:
time: 578 us; the launch traced here: 569 us
  waiting for transfers between devices  219 us (38%)
  Pallas kernels  89.8 us (16%)
  matrix products  77.2 us (13%)
  other arithmetic  73.4 us (13%)
  starting transfers between devices  50.7 us (9%)
  local copies, waits for them, and re-layouts  43.3 us (7%)
  between operations  16.5 us (3%)
    dot_general x22, matrix products, contract(): lax.dot_general(left, right, (((left_axis,), (right_axis,)), ((), ())), p...  77.2 us
    ppermute x8, waiting for transfers between devices, swap_near(): return lax.ppermute(value, 'z', [(0, 1), (1, 0), (2, 3), (3, 2)])  60.3 us
    ppermute x34, waiting for transfers between devices, swap(): return lax.ppermute(value, axis, [(0, 1), (1, 0)])  55 us
    ppermute x4, waiting for transfers between devices, swap_far(): return lax.ppermute(value, 'z', [(0, 2), (2, 0), (1, 3), (3, 1)])  45.5 us
    pallas_call x1, Pallas kernels, attend_backward(): pl.pallas_call(functools.partial(backward_kernel, size=size, count=count)...  33.9 us
    pallas_call x1, Pallas kernels, attend_forward(): pl.pallas_call(functools.partial(forward_kernel, size=size, count=count),...  26.2 us
    unnamed x167, local copies, waits for them, and re-layouts  24.2 us
    ppermute x34, starting transfers between devices, swap(): return lax.ppermute(value, axis, [(0, 1), (1, 0)])  22.5 us
  transfers between devices with their start and end apart: 58, of which 26 were waited for; matrix products, arithmetic and copies ran while one was open for 29% of the time, Pallas kernels for 15%

commit v1 on v0

--- a/solution.py
+++ b/solution.py
@@ -28,11 +28,15 @@
     )
 
 
-def visible(first, second, query_block, key_block, size):
-    key = key_block * size + lax.broadcasted_iota(jnp.int32, (size, size), 0)
-    query = query_block * size + lax.broadcasted_iota(jnp.int32, (1, size), 1)
+def visible(first, second, query_start, key_start, queries, keys):
+    key = key_start + lax.broadcasted_iota(jnp.int32, (keys, queries), 0)
+    query = query_start + lax.broadcasted_iota(jnp.int32, (1, queries), 1)
     start = jnp.where(query >= second, second, jnp.where(query >= first, first, 0))
     return (key >= start) & (key <= query)
+
+
+def halves_of(size):
+    return slice(0, size // 2), slice(size // 2, size)
 
 
 def slot_of(block, count):
@@ -78,16 +82,24 @@
     mixed_s[...] = jnp.zeros_like(mixed_s)
 
     def add_block(block, masked):
-        scores = contract(key_s[block], query, 1, 0)
-        if masked:
-            scores = jnp.where(visible(first, second, here, block, size), scores, NEG)
-        old_top = top_s[...]
-        top = jnp.maximum(old_top, jnp.max(scores, 0, keepdims=True))
-        expo = jnp.exp2(scores - top)
-        scale = jnp.exp2(old_top - top)
-        top_s[...] = top
-        total_s[...] = total_s[...] * scale + jnp.sum(expo, 0, keepdims=True)
-        mixed_s[...] = mixed_s[...] * scale + contract(value_s[block], expo.astype(LOW), 1, 0)
+        keys, values = key_s[block], value_s[block]
+        parts = halves_of(size)
+        all_scores = [contract(keys, query[:, part], 1, 0) for part in parts]
+        for part, scores in zip(parts, all_scores):
+            if masked:
+                seen = visible(
+                    first, second, here * size + part.start, block * size, size // 2, size
+                )
+                scores = jnp.where(seen, scores, NEG)
+            old_top = top_s[:, part]
+            top = jnp.maximum(old_top, jnp.max(scores, 0, keepdims=True))
+            expo = jnp.exp2(scores - top)
+            scale = jnp.exp2(old_top - top)
+            top_s[:, part] = top
+            total_s[:, part] = total_s[:, part] * scale + jnp.sum(expo, 0, keepdims=True)
+            mixed_s[:, part] = mixed_s[:, part] * scale + contract(
+                values, expo.astype(LOW), 1, 0
+            )
 
     last = count - 1
 
@@ -156,15 +168,23 @@
     def add_block(block, masked):
         query = query_s[block]
         grad = grad_ref[slot_of(block, count)]
-        scores = contract(key_rows, query, 1, 0)
-        if masked:
-            scores = jnp.where(visible(first, second, block, here, size), scores, NEG)
-        probs = jnp.exp2(scores - log_ref[block])
-        grad_probs = contract(value_rows, grad, 1, 0)
-        grad_scores = (probs * (grad_probs - delta_s[block])).astype(LOW)
-        value_grad_s[...] += contract(grad, probs.astype(LOW), 1, 1)
-        key_grad_s[...] += contract(query, grad_scores, 1, 1)
-        query_grad_s[block] += contract(key, grad_scores, 1, 0)
+        log_total, delta = log_ref[block], delta_s[block]
+        parts = halves_of(size)
+        products = [
+            (contract(key_rows, query[:, part], 1, 0), contract(value_rows, grad[:, part], 1, 0))
+            for part in parts
+        ]
+        for part, (scores, grad_probs) in zip(parts, products):
+            if masked:
+                seen = visible(
+                    first, second, block * size + part.start, here * size, size // 2, size
+                )
+                scores = jnp.where(seen, scores, NEG)
+            probs = jnp.exp2(scores - log_total[:, part])
+            grad_scores = (probs * (grad_probs - delta[:, part])).astype(LOW)
+            value_grad_s[...] += contract(grad[:, part], probs.astype(LOW), 1, 1)
+            key_grad_s[...] += contract(query[:, part], grad_scores, 1, 1)
+            query_grad_s[block, :, part] += contract(key, grad_scores, 1, 0)
 
     last = count - 1
 
@@ -822,8 +842,9 @@
     gate_sum = gate_grad + gate_far
     gate_near = swap_near(gate_sum)
     block_output = (own_middle + feed_own + feed_near.astype(F32)).astype(LOW)[None]
-    came, up_far, gate_near, block_output, output_grad = tie(
-        swap(leaving, "x"), up_far, gate_near, block_output, output_grad
+    output_came = swap_near(output_grad)
+    came, up_far, gate_near, block_output, output_grad, output_came = tie(
+        swap(leaving, "x"), up_far, gate_near, block_output, output_grad, output_came
     )
 
     qkv_low, by_line = merge(scalars, kept, came, cosine, sine, lines)
@@ -835,19 +856,18 @@
     up_sum = up_grad + up_far
     up_near = swap_near(up_sum)
     down_pieces = four(down_sum, down_near)
-    token_grads, qkv_grad, up_near, down_pieces = tie(
-        token_grads, qkv_grad, up_near, down_pieces
+    token_grads, qkv_grad, up_near, down_pieces, output_came = tie(
+        token_grads, qkv_grad, up_near, down_pieces, output_came
     )
     all_qkv = gather(qkv_grad, seq)
+    output_sum = output_grad + output_came
+    output_far = swap_far(output_sum)
 
     token_grads = token_grads.reshape(-1, chip_count)
     split = lead_w.shape[1]
     grad_one = contract(token_grads[:split], lead_w, 0, 1) + contract(
         token_grads[split:], tail_w, 0, 1
     )
-    grad_one, output_came = tie(grad_one, swap_near(output_grad))
-    output_sum = output_grad + output_came
-    output_far = swap_far(output_sum)
     grad_one = mine_of(grad_one) + swap(theirs_of(grad_one).astype(LOW), "c").astype(F32)
     grad_rows = own_unit_scale * (
         grad_one - own_unit * jnp.mean(grad_one * own_unit, -1, keepdims=True)

time: 578 us -> 582 us (level)
    unnamed x167 -> x171, local copies, waits for them, and re-layouts: 24.2 us -> 25.4 us
  transfers between devices with their start and end apart: 58 -> 58, of which waited for: 26 -> 24; matrix products, arithmetic and copies ran while one was open for 29% -> 29% of each run, Pallas kernels for 15% -> 14%
where the time goes in v1:
time: 582 us; the launch traced here: 573 us
  waiting for transfers between devices  222 us (38%)
  Pallas kernels  87 us (15%)
  matrix products  77.2 us (13%)
  other arithmetic  72.5 us (12%)
  starting transfers between devices  53.5 us (9%)
  local copies, waits for them, and re-layouts  44.6 us (8%)
  between operations  16.5 us (3%)
    dot_general x22, matrix products, contract(): lax.dot_general(left, right, (((left_axis,), (right_axis,)), ((), ())), p...  77.2 us
    ppermute x8, waiting for transfers between devices, swap_near(): return lax.ppermute(value, 'z', [(0, 1), (1, 0), (2, 3), (3, 2)])  61 us
    ppermute x34, waiting for transfers between devices, swap(): return lax.ppermute(value, axis, [(0, 1), (1, 0)])  49.5 us
    ppermute x4, waiting for transfers between devices, swap_far(): return lax.ppermute(value, 'z', [(0, 2), (2, 0), (1, 3), (3, 1)])  49.2 us
    pallas_call x1, Pallas kernels, attend_backward(): pl.pallas_call(functools.partial(backward_kernel, size=size, count=count)...  31.7 us
    pallas_call x1, Pallas kernels, attend_forward(): pl.pallas_call(functools.partial(forward_kernel, size=size, count=count),...  25.7 us
    unnamed x171, local copies, waits for them, and re-layouts  25.4 us
    reduce_scatter x3, waiting for transfers between devices, fast_body(): lax.psum_scatter(value, fsdp, scatter_dimension=0, tiled=True)  24.2 us
  transfers between devices with their start and end apart: 58, of which 24 were waited for; matrix products, arithmetic and copies ran while one was open for 29% of the time, Pallas kernels for 14%

profile of v1, /device:TPU:0, one launch (start us, length us, event | category | flops | bytes accessed | tf_op | source)
XLA Modules:
  0.0 572.8 jit_solution(1589355922508325462)
XLA Ops:
  27.8 13.6 %collective-permute-done.1 = bf16[384,1024]{1,0:T(8,128)(2,1)} collective-permute-done((bf16[384,1024]{1,0:T(8,128)(2,1)}, bf16[384,1024]{1,0:T(8,128)(2,1)}, u32[]{:S(2)}, u32[]{:S(2)}) %collective-permute-start.1) | collective-permute-done | bytes 786464 | tf_op jit(solution)/shard_map/ppermute | solution.py:560
  53.5 9.7 %collective-permute-done.3 = bf16[2,384,384]{2,1,0:T(8,128)(2,1)S(1)} collective-permute-done((bf16[2,384,384]{2,1,0:T(8,128)(2,1)S(1)}, bf16[2,384,384]{2,1,0:T(8,128)(2,1)S(1)}, u32[]{:S(2)}, u32[]{:S(2)}) %collective-permute-start.3) | collective-permute-done | bytes 589856 | tf_op jit(solution)/shard_map/ppermute | solution.py:560
  64.5 14.1 %all-gather.7.cloned.1.call-done = bf16[2048,1536]{1,0:T(8,128)(2,1)} async-done(((bf16[256,1536]{1,0:T(8,128)(2,1)}), bf16[2048,1536]{1,0:T(8,128)(2,1)}) %all-gather.7.cloned.1.call-update) | async-done | bytes 6291472 | tf_op jit(solution)/shard_map/all_gather | solution.py:657
  78.9 5.2 fusion.39.lin_ref
  95.3 15.6 %collective-permute-done.6 = bf16[256,1536]{1,0:T(8,128)(2,1)} collective-permute-done((bf16[256,1536]{1,0:T(8,128)(2,1)}, bf16[256,1536]{1,0:T(8,128)(2,1)}, u32[]{:S(2)}, u32[]{:S(2)}) %collective-permute-start.6) | collective-permute-done | bytes 786464 | tf_op jit(solution)/shard_map/ppermute | solution.py:564
  110.9 5.4 collective-permute-done.5.other_ref
  121.6 25.7 %attend_forward.1 = (bf16[8,96,512]{2,1,0:T(8,128)(2,1)S(1)}, f32[8,96,512]{2,1,0:T(8,128)S(1)}, f32[8,1,512]{2,1,0:T(1,128)S(1)}) custom-call(s32[4]{0:T(128)S(1)} %pad_add_fusion.scalars, bf16[288,2048]{1,0:T(8,128)(2,1)S(1)} %copy-done.34, bf16[288,2048]{1,0:T(8,128)(2,1)} %collective-permute-done.5.other_ref), custom_call_target="tpu_custom_call" | custom-call | flops 28991029248 | bytes 10485760 | tf_op jit(solution)/shard_map/attend_forward/pallas_call | solution.py:220
  163.8 9.0 %all-to-all-done = bf16[8,96,512]{2,1,0:T(8,128)(2,1)} async-done(((bf16[8,96,512]{2,1,0:T(8,128)(2,1)}), bf16[8,96,512]{2,1,0:T(8,128)(2,1)}, u32[]{:S(2)}, u32[]{:S(2)}) %all-to-all-start) | async-done | bytes 786464 | tf_op jit(solution)/shard_map/all_to_all | solution.py:722
  194.6 6.1 %all-gather.11.cloned.1.call-done = bf16[1024,1536]{1,0:T(8,128)(2,1)} async-done(((bf16[256,1536]{1,0:T(8,128)(2,1)}), bf16[1024,1536]{1,0:T(8,128)(2,1)}) %all-gather.11.cloned.1.call-update) | async-done | bytes 3145744 | tf_op jit(solution)/shard_map/all_gather | solution.py:657
  200.8 6.2 %multiply_convert_fusion.4 = (bf16[512,1024]{1,0:T(8,128)(2,1)S(1)}, bf16[512,1024]{1,0:T(8,128)(2,1)S(1)}, bf16[512,1024]{1,0:T(8,128)(2,1)S(1)}) fusion(f32[512,1024]{1,0:T(8,128)} %fusion.41, f32[512,1024]{1,0:T(8,128)} %fusion.40, bf16[512,1536]{1,0:T(8,128)(2,1)} %pad_maximum_fusion.6, bf16[1024,1536]{1,0:T(8,128)(2,1)} %all-gather.11.cloned.1.call-done), kind=kOutput, calls=%fused_computation.32 | convolution fusion | flops 1618477056 | bytes 12058624 | tf_op jit(solution)/shard_map/dot_general | solution.py:26
  239.0 6.3 %convolution_convert_fusion.1 = bf16[1536,1024]{1,0:T(8,128)(2,1)} fusion(bf16[512,1024]{1,0:T(8,128)(2,1)S(1)} %get-tuple-element.131, bf16[512,1024]{1,0:T(8,128)(2,1)S(1)} %get-tuple-element.202, bf16[256,1536]{1,0:T(8,128)(2,1)S(1)} %collective-permute-done.14, bf16[256,1536]{1,0:T(8,128)(2,1)} %collective-permute-done.13, ...), kind=kOutput, calls=%fused_computation.1 | convolution fusion | flops 3236429824 | bytes 8388608 | tf_op jit(solution)/shard_map/dot_general | solution.py:26
  245.2 7.4 %convolution_convert_fusion = bf16[1536,1024]{1,0:T(8,128)(2,1)} fusion(bf16[512,1024]{1,0:T(8,128)(2,1)} %copy-done.84, bf16[512,1024]{1,0:T(8,128)(2,1)} %copy-done.83, bf16[256,1536]{1,0:T(8,128)(2,1)} %copy-done.65, bf16[256,1536]{1,0:T(8,128)(2,1)} %collective-permute-done.13, bf16[512,1536]{1,0:T(8,128)(2,1)S(1)} %copy-done.48), kind=kOutput, calls=%fused_computation | convolution fusion | flops 3236429824 | bytes 8388608 | tf_op jit(solution)/shard_map/dot_general | solution.py:26
  285.2 29.1 %collective-permute-done.23 = bf16[256,1536]{1,0:T(8,128)(2,1)S(1)} collective-permute-done((bf16[256,1536]{1,0:T(8,128)(2,1)S(1)}, bf16[256,1536]{1,0:T(8,128)(2,1)S(1)}, u32[]{:S(2)}, u32[]{:S(2)}) %collective-permute-start.23) | collective-permute-done | bytes 786464 | tf_op jit(solution)/shard_map/ppermute | solution.py:568
  315.1 4.8 all-to-all-start.1
  332.6 7.8 %all-to-all-done.1.grad_ref = bf16[8,96,512]{2,1,0:T(8,128)(2,1)S(1)} async-done(((bf16[8,96,512]{2,1,0:T(8,128)(2,1)}), bf16[8,96,512]{2,1,0:T(8,128)(2,1)S(1)}, u32[]{:S(2)}, u32[]{:S(2)}) %all-to-all-start.1) | async-done | bytes 786464 | tf_op jit(solution)/shard_map/all_to_all | solution.py:722
  345.5 31.7 %attend_backward.1 = (bf16[288,2048]{1,0:T(8,128)(2,1)S(1)}, bf16[288,2048]{1,0:T(8,128)(2,1)S(1)}) custom-call(s32[4]{0:T(128)S(1)} %pad_add_fusion.scalars, bf16[288,2048]{1,0:T(8,128)(2,1)S(1)} %copy-done.34, bf16[288,2048]{1,0:T(8,128)(2,1)} %collective-permute-done.5.other_ref, bf16[8,96,512]{2,1,0:T(8,128)(2,1)S(1)} %copy-done.29, ...), custom_call_target="tpu_custom_call" | custom-call | flops 38050725888 | bytes 16777216 | tf_op jit(solution)/shard_map/attend_backward/pallas_call | solution.py:264
  379.2 8.1 %collective-permute-done.25.refs_2_ = bf16[256,1536]{1,0:T(8,128)(2,1)} collective-permute-done((bf16[256,1536]{1,0:T(8,128)(2,1)}, bf16[256,1536]{1,0:T(8,128)(2,1)}, u32[]{:S(2)}, u32[]{:S(2)}) %collective-permute-start.25) | collective-permute-done | bytes 786464 | tf_op jit(solution)/shard_map/ppermute | solution.py:564
  393.8 24.2 %reduce-scatter.8.cloned.1.call-done = bf16[192,1536]{1,0:T(8,128)(2,1)} async-done(((bf16[768,1536]{1,0:T(8,128)(2,1)}), bf16[192,1536]{1,0:T(8,128)(2,1)}) %reduce-scatter.8.cloned.1.call-update) | async-done | bytes 589840 | tf_op jit(solution)/shard_map/reduce_scatter | solution.py:771
  423.1 17.0 %collective-permute-done.31 = bf16[192,1536]{1,0:T(8,128)(2,1)S(1)} collective-permute-done((bf16[192,1536]{1,0:T(8,128)(2,1)}, bf16[192,1536]{1,0:T(8,128)(2,1)S(1)}, u32[]{:S(2)}, u32[]{:S(2)}) %collective-permute-start.31) | collective-permute-done | bytes 589856 | tf_op jit(solution)/shard_map/ppermute | solution.py:564
  452.9 6.3 %convolution_convert_fusion.5 = bf16[1536,384]{1,0:T(8,128)(2,1)S(1)} fusion(bf16[2048,1536]{1,0:T(8,128)(2,1)} %all-gather.7.cloned.1.call-done, bf16[384,2048]{1,0:T(8,128)(2,1)S(1)} %get-tuple-element.169), kind=kOutput, calls=%fused_computation.16 | convolution fusion | flops 2416508928 | bytes 9043968 | tf_op jit(solution)/shard_map/dot_general | solution.py:26
  477.4 19.2 %collective-permute-done.36.refs_6_ = bf16[384,1024]{1,0:T(8,128)(2,1)} collective-permute-done((bf16[384,1024]{1,0:T(8,128)(2,1)}, bf16[384,1024]{1,0:T(8,128)(2,1)}, u32[]{:S(2)}, u32[]{:S(2)}) %collective-permute-start.36) | collective-permute-done | bytes 786464 | tf_op jit(solution)/shard_map/ppermute | solution.py:564
  513.4 6.4 %place_rows.3 = f32[1024,1536]{1,0:T(8,128)} custom-call(s32[4]{0:T(128)S(1)} %pad_add_fusion.1.order, bf16[256,1536]{1,0:T(8,128)(2,1)} %fusion.32.refs_0_, bf16[256,1536]{1,0:T(8,128)(2,1)S(1)} %copy-done.23, bf16[256,1536]{1,0:T(8,128)(2,1)} %collective-permute-done.25.refs_2_, bf16[256,1536]{1,0:T(8,128)(2,1)S(1)} %copy-done.25), custom_call_target="tpu_custom_call" | custom-call | bytes 9437184 | tf_op jit(solution)/shard_map/place_rows/pallas_call | solution.py:312
  519.8 9.4 %place_columns.1 = (f32[384,4096]{1,0:T(8,128)}, f32[384,4096]{1,0:T(8,128)}, f32[384,1]{1,0:T(8,128)S(1)}) custom-call(s32[4]{0:T(128)S(1)} %pad_add_fusion.1.order, f32[384,1]{1,0:T(8,128)S(1)} %broadcast_in_dim.31.gain_ref, bf16[384,4096]{1,0:T(8,128)(2,1)S(1)} %copy-done.5, bf16[384,4096]{1,0:T(8,128)(2,1)S(1)} %copy-done.4, ...), custom_call_target="tpu_custom_call" | custom-call | flops 9437184 | bytes 25165824 | tf_op jit(solution)/shard_map/place_columns/pallas_call | solution.py:358
  531.3 20.1 %collective-permute-done.40 = bf16[192,1536]{1,0:T(8,128)(2,1)} collective-permute-done((bf16[192,1536]{1,0:T(8,128)(2,1)}, bf16[192,1536]{1,0:T(8,128)(2,1)}, u32[]{:S(2)}, u32[]{:S(2)}) %collective-permute-start.40) | collective-permute-done | bytes 589856 | tf_op jit(solution)/shard_map/ppermute | solution.py:568
  (391 shorter events, 248.1 us)
Async XLA Ops:
  7.2 71.4 %all-gather.7.cloned.1.call-start = ((), (), s32[]{:S(2)}) async-start(), calls=%async_computation.6 | async-start | bytes 7077888 | tf_op jit(solution)/shard_map/all_gather | solution.py:657
  11.0 161.7 %all-gather.9.cloned.1.call-start = ((), (), s32[]{:S(2)}) async-start(), calls=%async_computation.7 | async-start | bytes 2949120 | tf_op jit(solution)/shard_map/all_gather | solution.py:657
  48.8 46.5 %collective-permute-start.8 = (bf16[2,384,1024]{2,1,0:T(8,128)(2,1)}, bf16[2,384,1024]{2,1,0:T(8,128)(2,1)}, u32[]{:S(2)}, u32[]{:S(2)}) collective-permute-start(bf16[2,384,1024]{2,1,0:T(8,128)(2,1)} %pad_maximum_fusion.3), channel_id=1, source_target_pairs={{0,2},{2,0},{1,3},{3,1},{4,6},{6,4},{5,7},{7,5},{8,10},{10,8},{9,1... | collective-permute-start | bytes 4718600 | tf_op jit(solution)/shard_map/ppermute | solution.py:560
  49.0 46.3 %collective-permute-start.9 = (bf16[2,384,1024]{2,1,0:T(8,128)(2,1)}, bf16[2,384,1024]{2,1,0:T(8,128)(2,1)}, u32[]{:S(2)}, u32[]{:S(2)}) collective-permute-start(bf16[2,384,1024]{2,1,0:T(8,128)(2,1)} %pad_maximum_fusion.4), channel_id=1, source_target_pairs={{0,1},{1,0},{2,3},{3,2},{4,5},{5,4},{6,7},{7,6},{8,9},{9,8},{10,11... | collective-permute-start | bytes 4718600 | tf_op jit(solution)/shard_map/ppermute | solution.py:560
  116.4 84.4 %all-gather.11.cloned.1.call-start = ((), (), s32[]{:S(2)}) async-start(), calls=%async_computation.8 | async-start | bytes 3932160 | tf_op jit(solution)/shard_map/all_gather | solution.py:657
  119.4 28.7 %collective-permute-start.10 = (bf16[256,1536]{1,0:T(8,128)(2,1)}, bf16[256,1536]{1,0:T(8,128)(2,1)}, u32[]{:S(2)}, u32[]{:S(2)}) collective-permute-start(bf16[256,1536]{1,0:T(8,128)(2,1)} %collective-permute-done.6), channel_id=1, source_target_pairs={{0,4},{4,0},{1,5},{5,1},{2,6},{6,2},{3,7},{7,3},{8,12},{12,8},{9,1... | collective-permute-start | bytes 2359304 | tf_op jit(solution)/shard_map/ppermute | solution.py:560
  152.4 117.6 %all-gather.13.cloned.1.call-start = ((), (), s32[]{:S(2)}) async-start(), calls=%async_computation.9 | async-start | bytes 2949120 | tf_op jit(solution)/shard_map/all_gather | solution.py:657
  177.3 163.9 %reduce-scatter.4.cloned.1.call-start = ((), (), s32[]{:S(2)}) async-start(), calls=%async_computation.10 | async-start | bytes 3932160 | tf_op jit(solution)/shard_map/reduce_scatter | solution.py:771
  212.9 51.9 %collective-permute-start.12 = (bf16[256,1536]{1,0:T(8,128)(2,1)}, bf16[256,1536]{1,0:T(8,128)(2,1)}, u32[]{:S(2)}, u32[]{:S(2)}) collective-permute-start(bf16[256,1536]{1,0:T(8,128)(2,1)} %dynamic-slice_convert_fusion.2), channel_id=1, source_target_pairs={{0,4},{4,0},{1,5},{5,1},{2,6},{6,2},{3,7},{7,3},{8,12},{12,8},{9,1... | collective-permute-start | bytes 2359304 | tf_op jit(solution)/shard_map/ppermute | solution.py:560
  274.6 114.2 %reduce-scatter.6.cloned.1.call-start = ((), (), s32[]{:S(2)}) async-start(), calls=%async_computation.11 | async-start | bytes 3932160 | tf_op jit(solution)/shard_map/reduce_scatter | solution.py:771
  276.8 37.4 %collective-permute-start.23 = (bf16[256,1536]{1,0:T(8,128)(2,1)S(1)}, bf16[256,1536]{1,0:T(8,128)(2,1)S(1)}, u32[]{:S(2)}, u32[]{:S(2)}) collective-permute-start(bf16[256,1536]{1,0:T(8,128)(2,1)S(1)} %pad_maximum_fusion.12), channel_id=1, source_target_pairs={{0,16},{16,0},{8,24},{24,8},{1,17},{17,1},{9,25},{25,9},{2,18},{18... | collective-permute-start | bytes 2359304 | tf_op jit(solution)/shard_map/ppermute | solution.py:568
  319.9 98.1 %reduce-scatter.8.cloned.1.call-start = ((), (), s32[]{:S(2)}) async-start(), calls=%async_computation.12 | async-start | bytes 2949120 | tf_op jit(solution)/shard_map/reduce_scatter | solution.py:771
  324.4 175.9 %all-gather.15.cloned.1.call-start = ((), (), s32[]{:S(2)}) async-start(), calls=%async_computation.13 | async-start | bytes 2949120 | tf_op jit(solution)/shard_map/all_gather | solution.py:657
  329.5 90.0 %collective-permute-start.30 = (bf16[256,1536]{1,0:T(8,128)(2,1)}, bf16[256,1536]{1,0:T(8,128)(2,1)}, u32[]{:S(2)}, u32[]{:S(2)}) collective-permute-start(bf16[256,1536]{1,0:T(8,128)(2,1)} %dynamic-slice_convert_fusion.1), channel_id=1, source_target_pairs={{0,4},{4,0},{1,5},{5,1},{2,6},{6,2},{3,7},{7,3},{8,12},{12,8},{9,1... | collective-permute-start | bytes 2359304 | tf_op jit(solution)/shard_map/ppermute | solution.py:560
  329.5 49.7 %collective-permute-start.26 = (bf16[256,1536]{1,0:T(8,128)(2,1)}, bf16[256,1536]{1,0:T(8,128)(2,1)}, u32[]{:S(2)}, u32[]{:S(2)}) collective-permute-start(bf16[256,1536]{1,0:T(8,128)(2,1)} %fusion.23), channel_id=1, source_target_pairs={{0,8},{8,0},{16,24},{24,16},{1,9},{9,1},{17,25},{25,17},{2,10},{10... | collective-permute-start | bytes 2359304 | tf_op jit(solution)/shard_map/ppermute | solution.py:564
  341.3 37.9 %collective-permute-start.24 = (bf16[384,1024]{1,0:T(8,128)(2,1)}, bf16[384,1024]{1,0:T(8,128)(2,1)}, u32[]{:S(2)}, u32[]{:S(2)}) collective-permute-start(bf16[384,1024]{1,0:T(8,128)(2,1)} %reduce-scatter.4.cloned.1.call-done), channel_id=1, source_target_pairs={{0,16},{16,0},{8,24},{24,8},{1,17},{17,1},{9,25},{25,9},{2,18},{18... | collective-permute-start | bytes 2359304 | tf_op jit(solution)/shard_map/ppermute | solution.py:568
  341.3 46.1 %collective-permute-start.25 = (bf16[256,1536]{1,0:T(8,128)(2,1)}, bf16[256,1536]{1,0:T(8,128)(2,1)}, u32[]{:S(2)}, u32[]{:S(2)}) collective-permute-start(bf16[256,1536]{1,0:T(8,128)(2,1)} %fusion.32.refs_0_), channel_id=1, source_target_pairs={{0,8},{8,0},{16,24},{24,16},{1,9},{9,1},{17,25},{25,17},{2,10},{10... | collective-permute-start | bytes 2359304 | tf_op jit(solution)/shard_map/ppermute | solution.py:564
  387.3 53.9 %collective-permute-start.27 = (bf16[288,2048]{1,0:T(8,128)(2,1)}, bf16[288,2048]{1,0:T(8,128)(2,1)S(1)}, u32[]{:S(2)}, u32[]{:S(2)}) collective-permute-start(bf16[288,2048]{1,0:T(8,128)(2,1)} %copy-done.35), channel_id=1, source_target_pairs={{0,1},{1,0},{2,3},{3,2},{4,5},{5,4},{6,7},{7,6},{8,9},{9,8},{10,11... | collective-permute-start | bytes 3538952 | tf_op jit(solution)/shard_map/ppermute | solution.py:560
  388.8 51.4 %collective-permute-start.28 = (bf16[384,1024]{1,0:T(8,128)(2,1)}, bf16[384,1024]{1,0:T(8,128)(2,1)S(1)}, u32[]{:S(2)}, u32[]{:S(2)}) collective-permute-start(bf16[384,1024]{1,0:T(8,128)(2,1)} %reduce-scatter.6.cloned.1.call-done), channel_id=1, source_target_pairs={{0,16},{16,0},{8,24},{24,8},{1,17},{17,1},{9,25},{25,9},{2,18},{18... | collective-permute-start | bytes 2359304 | tf_op jit(solution)/shard_map/ppermute | solution.py:568
  391.5 48.7 %collective-permute-start.29 = (bf16[384,1024]{1,0:T(8,128)(2,1)S(1)}, bf16[384,1024]{1,0:T(8,128)(2,1)}, u32[]{:S(2)}, u32[]{:S(2)}) collective-permute-start(bf16[384,1024]{1,0:T(8,128)(2,1)S(1)} %add.291.refs_0_), channel_id=1, source_target_pairs={{0,8},{8,0},{16,24},{24,16},{1,9},{9,1},{17,25},{25,17},{2,10},{10... | collective-permute-start | bytes 2359304 | tf_op jit(solution)/shard_map/ppermute | solution.py:564
  448.1 48.5 %all-to-all-start.2 = ((bf16[4,384,512]{2,1,0:T(8,128)(2,1)}), bf16[4,384,512]{2,1,0:T(8,128)(2,1)}, u32[]{:S(2)}, u32[]{:S(2)}) async-start(bf16[4,384,512]{2,1,0:T(8,128)(2,1)} %get-tuple-element.168), calls=%async_computation.5 | async-start | bytes 3145728 | tf_op jit(solution)/shard_map/all_to_all | solution.py:851
  452.5 98.9 %all-gather.17.cloned.1.call-start = ((), (), s32[]{:S(2)}) async-start(), calls=%async_computation.14 | async-start | bytes 2654208 | tf_op jit(solution)/shard_map/all_gather | solution.py:657
  463.5 33.1 %collective-permute-start.36 = (bf16[384,1024]{1,0:T(8,128)(2,1)}, bf16[384,1024]{1,0:T(8,128)(2,1)}, u32[]{:S(2)}, u32[]{:S(2)}) collective-permute-start(bf16[384,1024]{1,0:T(8,128)(2,1)} %add.299.refs_4_), channel_id=1, source_target_pairs={{0,8},{8,0},{16,24},{24,16},{1,9},{9,1},{17,25},{25,17},{2,10},{10... | collective-permute-start | bytes 2359304 | tf_op jit(solution)/shard_map/ppermute | solution.py:564
  508.4 43.0 %collective-permute-start.40 = (bf16[192,1536]{1,0:T(8,128)(2,1)}, bf16[192,1536]{1,0:T(8,128)(2,1)}, u32[]{:S(2)}, u32[]{:S(2)}) collective-permute-start(bf16[192,1536]{1,0:T(8,128)(2,1)} %add.303), channel_id=1, source_target_pairs={{0,16},{16,0},{8,24},{24,8},{1,17},{17,1},{9,25},{25,9},{2,18},{18... | collective-permute-start | bytes 1769480 | tf_op jit(solution)/shard_map/ppermute | solution.py:568
  (119 other events, 1162.1 us)
Sparse Core Ops, SparseCore 0:
  11.2 67.4 all-gather.6
  116.5 36.1 all-gather.8
  155.1 45.5 all-gather.10
  202.4 43.8 all-gather.12
  274.7 43.9 reduce-scatter.3
  321.5 46.3 reduce-scatter.5
  371.5 46.4 reduce-scatter.7
  419.8 37.4 all-gather.14
  496.7 50.0 all-gather.16
